TPU v7x, 32 devices: a whole 2x2x4 slice. The times are simulated.
32 devices in a mesh: dp: 8 (over z, core), ctx: 4 (over y, x).
Axes of the slice: x: 2, y: 2, z: 4, core: 2. Of those that a mesh axis runs over, the one named last changes fastest.
Arguments:
- tokens: bfloat16 [8, 512, 2048], P('dp', 'ctx'), may hold values from -6 to 6
- cotangent: bfloat16 [8, 512, 2048], P('dp', 'ctx'), may hold values from -6 to 6
- pair_index: int32 [4], replicated, may hold values from 0 to 3, each once
- norm1_gain: bfloat16 [2048], P('dp'), may hold values from 0.25 to 1.75
- norm1_bias: bfloat16 [2048], P('dp'), may hold values from -1.75 to 1.75
- norm2_gain: bfloat16 [2048], P('dp'), may hold values from 0.25 to 1.75
- norm2_bias: bfloat16 [2048], P('dp'), may hold values from -1.75 to 1.75
- w_qkv: bfloat16 [2048, 6144], P('dp'), may hold values from -0.1875 to 0.1875
- b_qkv: bfloat16 [6144], P('dp'), may hold values from -1.75 to 1.75
- w_out: bfloat16 [2048, 2048], P('dp'), may hold values from -0.375 to 0.375
- b_out: bfloat16 [2048], P('dp'), may hold values from -1.75 to 1.75
- w_up: bfloat16 [2048, 8192], P('dp'), may hold values from -0.125 to 0.125
- b_up: bfloat16 [8192], P('dp'), may hold values from -1.75 to 1.75
- w_down: bfloat16 [8192, 2048], P('dp'), may hold values from -0.0625 to 0.0625
- b_down: bfloat16 [2048], P('dp'), may hold values from -1.75 to 1.75
Outputs:
- output: bfloat16 [8, 512, 2048], P('dp', 'ctx')
- input_grad: bfloat16 [8, 512, 2048], P('dp', 'ctx')
- grad_norm1_gain: float32 [2048], P('dp')
- grad_norm1_bias: float32 [2048], P('dp')
- grad_norm2_gain: float32 [2048], P('dp')
- grad_norm2_bias: float32 [2048], P('dp')
- grad_w_qkv: float32 [2048, 6144], P('dp')
- grad_b_qkv: float32 [6144], P('dp')
- grad_w_out: float32 [2048, 2048], P('dp')
- grad_b_out: float32 [2048], P('dp')
- grad_w_up: float32 [2048, 8192], P('dp')
- grad_b_up: float32 [8192], P('dp')
- grad_w_down: float32 [8192, 2048], P('dp')
- grad_b_down: float32 [2048], P('dp')
Inputs may be any that keep to these rules, and one draw needn't show every extreme that they name: A permutation: index c of ctx holds the blocks pair_index[c] and 7 - pair_index[c] of the 8 blocks of 64 tokens of every sequence.
All inputs are finite; a program needn't handle non-finite values.
Results may differ from a plain program's by a relative error of at most 0.018.
Values may be sent and summed in bfloat16 or wider, within the bound.
A program may use at most 512 MiB of HBM per device.

v0:
```python
import jax
import jax.numpy as jnp
from jax import lax
from jax.sharding import PartitionSpec as P

H = 8
DH = 256
ROT = 64


EPS_NORM = 1e-05
ROPE_BASE = 10000.0
MASK_FILL = -1000000000.0


def shortened(x):

    def short(part):
        return part.astype(jnp.bfloat16) if part.dtype == jnp.float32 else part

    return jax.tree.map(short, x)


def layer_norm(values_in, gain_vec, offset):
    centre = values_in - jnp.mean(values_in, axis=-1, keepdims=True)
    spread = jnp.mean(centre * centre, axis=-1, keepdims=True)
    return centre * lax.rsqrt(spread + EPS_NORM) * gain_vec + offset


def norm_grads(values_in, gain_vec, offset, upstream):
    unused, pullback = jax.vjp(layer_norm, values_in, gain_vec, offset)
    return pullback(upstream)


def positions(pair_index, tok_count):
    ranks_total = pair_index.shape[0]
    half_len = tok_count // 2
    index_all = jnp.arange(ranks_total * tok_count, dtype=jnp.int32)
    owner_rank = index_all // tok_count
    within = index_all % tok_count
    match_table = owner_rank[:, None] == jnp.arange(ranks_total, dtype=jnp.int32)[None, :]
    first_block = jnp.sum(jnp.where(match_table, pair_index[None, :], 0), axis=1)
    block_id = jnp.where(within < half_len, first_block, 2 * ranks_total - 1 - first_block)
    return block_id * half_len + within % half_len


def rotary(head_vals, token_place, turn_sign):
    half_rot = ROT // 2
    frequency = ROPE_BASE ** (-2.0 * jnp.arange(half_rot, dtype=jnp.float32) / ROT)
    angles = token_place.astype(jnp.float32)[:, None] * frequency[None, :]
    cosine = jnp.cos(angles)[:, None, :]
    sine_part = turn_sign * jnp.sin(angles)[:, None, :]
    first_half = head_vals[..., :half_rot]
    second = head_vals[..., half_rot:ROT]
    return jnp.concatenate(
        [
            first_half * cosine - second * sine_part,
            second * cosine + first_half * sine_part,
            head_vals[..., ROT:],
        ],
        axis=-1,
    )


def contract_rows(left, right):
    return lax.dot_general(
        left, right, (((0,), (0,)), ((), ())), preferred_element_type=jnp.float32
    )


def contract_cols(left, right):
    return lax.dot_general(
        left, right, (((1,), (1,)), ((), ())), preferred_element_type=jnp.float32
    )


def local(
    tokens,
    cotangent,
    pair_index,
    norm1_gain,
    norm1_bias,
    norm2_gain,
    norm2_bias,
    w_qkv,
    b_qkv,
    w_out,
    b_out,
    w_up,
    b_up,
    w_down,
    b_down,
):
    seq_dev, tok_count, width = tokens.shape
    row_count = seq_dev * tok_count
    head_shape = (seq_dev, tok_count, H, DH)
    score_scale = DH ** (-0.5)
    device_rank = lax.axis_index("ctx")
    all_place = positions(pair_index, tok_count)
    own_place = lax.dynamic_slice_in_dim(all_place, device_rank * tok_count, tok_count)
    allowed = all_place[None, None, None, :] <= own_place[None, None, :, None]
    gathered = (
        lax.all_gather(norm1_gain, "dp", axis=0, tiled=True),
        lax.all_gather(norm1_bias, "dp", axis=0, tiled=True),
        lax.all_gather(norm2_gain, "dp", axis=0, tiled=True),
        lax.all_gather(norm2_bias, "dp", axis=0, tiled=True),
        lax.all_gather(w_qkv, "dp", axis=0, tiled=True),
        lax.all_gather(b_qkv, "dp", axis=0, tiled=True),
        lax.all_gather(w_out, "dp", axis=0, tiled=True),
        lax.all_gather(b_out, "dp", axis=0, tiled=True),
        lax.all_gather(w_up, "dp", axis=0, tiled=True),
        lax.all_gather(b_up, "dp", axis=0, tiled=True),
        lax.all_gather(w_down, "dp", axis=0, tiled=True),
        lax.all_gather(b_down, "dp", axis=0, tiled=True),
    )
    (
        attn_gain,
        attn_shift,
        mlp_gain,
        mlp_shift,
        qkv_weight,
        qkv_bias,
        out_weight,
        out_bias,
        up_weight,
        up_bias,
        down_weight,
        down_bias,
    ) = gathered
    token_rows = tokens.reshape(row_count, width).astype(jnp.float32)
    normed_attn = layer_norm(
        token_rows, attn_gain.astype(jnp.float32), attn_shift.astype(jnp.float32)
    ).astype(jnp.bfloat16)
    normed_mlp = layer_norm(
        token_rows, mlp_gain.astype(jnp.float32), mlp_shift.astype(jnp.float32)
    ).astype(jnp.bfloat16)
    projected = jnp.dot(
        normed_attn, qkv_weight, preferred_element_type=jnp.float32
    ) + qkv_bias.astype(jnp.float32)
    queries = rotary(projected[:, :width].reshape(head_shape), own_place, 1.0).astype(jnp.bfloat16)
    key_local = (
        rotary(projected[:, width : 2 * width].reshape(head_shape), own_place, 1.0)
        .astype(jnp.bfloat16)
        .reshape(seq_dev, tok_count, width)
    )
    value_local = projected[:, 2 * width :].astype(jnp.bfloat16).reshape(seq_dev, tok_count, width)
    key_all, value_all = (
        lax.all_gather(key_local, "ctx", axis=1, tiled=True),
        lax.all_gather(value_local, "ctx", axis=1, tiled=True),
    )
    seq_len = key_all.shape[1]
    key_heads = key_all.reshape(seq_dev, seq_len, H, DH)
    value_heads = value_all.reshape(seq_dev, seq_len, H, DH)
    raw_scores = (
        jnp.einsum("sqhd,skhd->shqk", queries, key_heads, preferred_element_type=jnp.float32)
        * score_scale
    )
    raw_scores = jnp.where(allowed, raw_scores, MASK_FILL)
    row_max = jnp.max(raw_scores, axis=-1, keepdims=True)
    exponent = jnp.exp(raw_scores - row_max)
    row_total = jnp.sum(exponent, axis=-1, keepdims=True)
    log_norm = row_max + jnp.log(row_total)
    prob_low = (exponent / row_total).astype(jnp.bfloat16)
    attn_mixed = (
        jnp.einsum("shqk,skhd->sqhd", prob_low, value_heads, preferred_element_type=jnp.float32)
        .reshape(row_count, width)
        .astype(jnp.bfloat16)
    )
    attn_branch = jnp.dot(
        attn_mixed, out_weight, preferred_element_type=jnp.float32
    ) + out_bias.astype(jnp.float32)
    hidden_pre = jnp.dot(
        normed_mlp, up_weight, preferred_element_type=jnp.float32
    ) + up_bias.astype(jnp.float32)
    hidden = jax.nn.gelu(hidden_pre, approximate=False).astype(jnp.bfloat16)
    mlp_branch = jnp.dot(
        hidden, down_weight, preferred_element_type=jnp.float32
    ) + down_bias.astype(jnp.float32)
    output = (token_rows + attn_branch + mlp_branch).astype(jnp.bfloat16).reshape(tokens.shape)
    attn_gain, mlp_gain, qkv_weight, out_weight, up_weight, down_weight = (
        lax.all_gather(norm1_gain, "dp", axis=0, tiled=True),
        lax.all_gather(norm2_gain, "dp", axis=0, tiled=True),
        lax.all_gather(w_qkv, "dp", axis=0, tiled=True),
        lax.all_gather(w_out, "dp", axis=0, tiled=True),
        lax.all_gather(w_up, "dp", axis=0, tiled=True),
        lax.all_gather(w_down, "dp", axis=0, tiled=True),
    )
    grad_rows = cotangent.reshape(row_count, width)
    grad_wide = grad_rows.astype(jnp.float32)
    hidden_grad = contract_cols(grad_rows, down_weight)
    unused, gelu_pull = jax.vjp(
        lambda pre_value: jax.nn.gelu(pre_value, approximate=False), hidden_pre
    )
    pre_grad = gelu_pull(hidden_grad)[0].astype(jnp.bfloat16)
    normed_mlp_grad = contract_cols(pre_grad, up_weight)
    mlp_in_grad, mlp_gain_grad, mlp_shift_grad = norm_grads(
        token_rows, mlp_gain.astype(jnp.float32), mlp_shift.astype(jnp.float32), normed_mlp_grad
    )
    mlp_terms = (
        contract_rows(normed_mlp, pre_grad),
        jnp.sum(pre_grad.astype(jnp.float32), axis=0),
        contract_rows(hidden, grad_rows),
        jnp.sum(grad_wide, axis=0),
        mlp_gain_grad,
        mlp_shift_grad,
    )
    mlp_shares = (
        lax.psum_scatter(
            mlp_terms[0].astype(jnp.bfloat16), "dp", scatter_dimension=0, tiled=True
        ).astype(jnp.float32),
        lax.psum_scatter(
            mlp_terms[1].astype(jnp.bfloat16), "dp", scatter_dimension=0, tiled=True
        ).astype(jnp.float32),
        lax.psum_scatter(
            mlp_terms[2].astype(jnp.bfloat16), "dp", scatter_dimension=0, tiled=True
        ).astype(jnp.float32),
        lax.psum_scatter(
            mlp_terms[3].astype(jnp.bfloat16), "dp", scatter_dimension=0, tiled=True
        ).astype(jnp.float32),
        lax.psum_scatter(
            mlp_terms[4].astype(jnp.bfloat16), "dp", scatter_dimension=0, tiled=True
        ).astype(jnp.float32),
        lax.psum_scatter(
            mlp_terms[5].astype(jnp.bfloat16), "dp", scatter_dimension=0, tiled=True
        ).astype(jnp.float32),
    )
    mixed_grad = contract_cols(grad_rows, out_weight).astype(jnp.bfloat16).reshape(head_shape)
    again_scores = (
        jnp.einsum("sqhd,skhd->shqk", queries, key_heads, preferred_element_type=jnp.float32)
        * score_scale
    )
    again_scores = jnp.where(allowed, again_scores, MASK_FILL)
    attn_prob = jnp.exp(again_scores - log_norm)
    prob_again = attn_prob.astype(jnp.bfloat16)
    prob_grad = jnp.einsum(
        "sqhd,skhd->shqk", mixed_grad, value_heads, preferred_element_type=jnp.float32
    )
    row_dot = jnp.sum(prob_grad * attn_prob, axis=-1, keepdims=True)
    score_grad = (attn_prob * (prob_grad - row_dot)).astype(jnp.bfloat16)
    query_grad = (
        jnp.einsum("shqk,skhd->sqhd", score_grad, key_heads, preferred_element_type=jnp.float32)
        * score_scale
    )
    key_part = (
        jnp.einsum("shqk,sqhd->skhd", score_grad, queries, preferred_element_type=jnp.float32)
        * score_scale
    ).reshape(seq_dev, seq_len, width)
    value_part = jnp.einsum(
        "shqk,sqhd->skhd", prob_again, mixed_grad, preferred_element_type=jnp.float32
    ).reshape(seq_dev, seq_len, width)
    key_grad, value_grad = (
        lax.psum_scatter(
            key_part.astype(jnp.bfloat16), "ctx", scatter_dimension=1, tiled=True
        ).astype(jnp.float32),
        lax.psum_scatter(
            value_part.astype(jnp.bfloat16), "ctx", scatter_dimension=1, tiled=True
        ).astype(jnp.float32),
    )
    query_back = rotary(query_grad, own_place, -1.0).reshape(row_count, width)
    key_back = rotary(key_grad.reshape(head_shape), own_place, -1.0).reshape(row_count, width)
    proj_grad = jnp.concatenate(
        [query_back, key_back, value_grad.reshape(row_count, width)], axis=1
    ).astype(jnp.bfloat16)
    normed_attn_grad = contract_cols(proj_grad, qkv_weight)
    attn_in_grad, attn_gain_grad, attn_shift_grad = norm_grads(
        token_rows, attn_gain.astype(jnp.float32), attn_shift.astype(jnp.float32), normed_attn_grad
    )
    input_grad = (grad_wide + mlp_in_grad + attn_in_grad).astype(jnp.bfloat16).reshape(tokens.shape)
    attn_terms = (
        contract_rows(normed_attn, proj_grad),
        jnp.sum(proj_grad.astype(jnp.float32), axis=0),
        contract_rows(attn_mixed, grad_rows),
        attn_gain_grad,
        attn_shift_grad,
    )
    attn_shares = (
        lax.psum_scatter(
            attn_terms[0].astype(jnp.bfloat16), "dp", scatter_dimension=0, tiled=True
        ).astype(jnp.float32),
        lax.psum_scatter(
            attn_terms[1].astype(jnp.bfloat16), "dp", scatter_dimension=0, tiled=True
        ).astype(jnp.float32),
        lax.psum_scatter(
            attn_terms[2].astype(jnp.bfloat16), "dp", scatter_dimension=0, tiled=True
        ).astype(jnp.float32),
        lax.psum_scatter(
            attn_terms[3].astype(jnp.bfloat16), "dp", scatter_dimension=0, tiled=True
        ).astype(jnp.float32),
        lax.psum_scatter(
            attn_terms[4].astype(jnp.bfloat16), "dp", scatter_dimension=0, tiled=True
        ).astype(jnp.float32),
    )
    summed = jax.tree.map(
        lambda part: part.astype(jnp.float32), lax.psum(shortened(mlp_shares + attn_shares), "ctx")
    )
    (
        up_total,
        up_bias_total,
        down_total,
        bias_total,
        mlp_gain_total,
        mlp_shift_total,
        qkv_total,
        qkv_bias_total,
        out_total,
        attn_gain_total,
        attn_shift_total,
    ) = summed
    return (
        output,
        input_grad,
        attn_gain_total,
        attn_shift_total,
        mlp_gain_total,
        mlp_shift_total,
        qkv_total,
        qkv_bias_total,
        out_total,
        bias_total,
        up_total,
        up_bias_total,
        down_total,
        bias_total,
    )


def solution(mesh):
    placed = (
        P("dp", "ctx", None),
        P("dp", "ctx", None),
        P(),
        P("dp"),
        P("dp"),
        P("dp"),
        P("dp"),
        P("dp", None),
        P("dp"),
        P("dp", None),
        P("dp"),
        P("dp", None),
        P("dp"),
        P("dp", None),
        P("dp"),
    )
    return jax.shard_map(
        local,
        mesh=mesh,
        in_specs=placed,
        out_specs=(
            P("dp", "ctx", None),
            P("dp", "ctx", None),
            P("dp"),
            P("dp"),
            P("dp"),
            P("dp"),
            P("dp", None),
            P("dp"),
            P("dp", None),
            P("dp"),
            P("dp", None),
            P("dp"),
            P("dp", None),
            P("dp"),
        ),
        check_vma=False,
    )
```

profile of v0, /device:TPU:1, one launch (start us, length us, event | category | flops | bytes accessed | tf_op | source)
XLA Modules:
  0.0 2321.2 jit_solution(8560419846264205876)
XLA Ops:
  8.8 13.3 all-gather.2
  22.2 8.8 all-gather.1
  31.0 17.9 all-gather.3
  51.1 181.3 %all-gather.15.cloned.1.call-done = bf16[2048,6144]{1,0:T(8,128)(2,1)} async-done(((bf16[256,6144]{1,0:T(8,128)(2,1)}), bf16[2048,6144]{1,0:T(8,128)(2,1)}) %all-gather.15.cloned.1.call-update) | async-done | bytes 25165840 | tf_op jit(solution)/shard_map/all_gather | solution.py:107
  232.4 10.8 convolution_add_fusion.1
  245.5 1.1 fusion.55
  247.5 1.2 copy.88
  248.8 2.1 slice.93
  251.3 62.9 %all-gather.19.cloned.1.call-done = bf16[2048,2048]{1,0:T(8,128)(2,1)} async-done(((bf16[256,2048]{1,0:T(8,128)(2,1)}), bf16[2048,2048]{1,0:T(8,128)(2,1)}) %all-gather.19.cloned.1.call-update) | async-done | bytes 8388624 | tf_op jit(solution)/shard_map/all_gather | solution.py:109
  314.2 6.3 convolution_convert_fusion.4
  322.6 27.3 %all-gather.17.cloned.1.call-done = bf16[1,512,2048]{1,2,0:T(8,128)(2,1)} async-done(((bf16[1,128,2048]{1,2,0:T(8,128)(2,1)}), bf16[1,512,2048]{1,2,0:T(8,128)(2,1)}) %all-gather.17.cloned.1.call-update) | async-done | bytes 2097168 | tf_op jit(solution)/shard_map/all_gather | solution.py:148
  349.9 2.6 fusion.81
  353.2 34.3 %all-gather.25.cloned.1.call-done = bf16[512,2048]{1,0:T(8,128)(2,1)} async-done(((bf16[128,2048]{1,0:T(8,128)(2,1)}), bf16[512,2048]{1,0:T(8,128)(2,1)}) %all-gather.25.cloned.1.call-update) | async-done | bytes 2097168 | tf_op jit(solution)/shard_map/all_gather | solution.py:149
  387.6 2.7 multiply_reduce_fusion
  391.8 2.4 multiply_convert_fusion
  394.2 10.7 copy.103
  404.9 4.8 copy.152
  409.8 3.2 convolution_convert_fusion.5
  413.0 10.8 copy.105
  423.8 4.9 copy.151
  430.7 2.7 fusion.30
  434.2 5.7 convolution_convert_fusion.3
  440.0 1.2 copy-done.4
  441.2 2.4 fusion.18
  443.6 1.0 slice.91
  445.1 1.7 reshape_bitcast_fusion.1
  446.8 1.9 copy.104
  448.7 1.1 slice.79
  449.8 1.2 copy.96
  451.1 2.1 subtract_convert_fusion.1
  454.0 1.9 copy.98
  455.8 1.7 copy.97
  457.5 26.5 %reduce-scatter.21.cloned.1.call-done = bf16[128,2048]{1,0:T(8,128)(2,1)} async-done(((bf16[512,2048]{1,0:T(8,128)(2,1)}), bf16[128,2048]{1,0:T(8,128)(2,1)}) %reduce-scatter.21.cloned.1.call-update) | async-done | bytes 524304
  484.0 1.7 reshape_bitcast_fusion
  486.5 1.1 pad_maximum_fusion.4
  487.6 18.9 convolution_convert_fusion.2
  507.2 13.4 all-gather.6
  520.6 14.1 all-gather.5
  534.7 36.1 %all_gather.59 = bf16[8192]{0:T(1024)(128)(2,1)S(1)} all-gather(bf16[1024]{0:T(1024)(128)(2,1)S(1)} %copy-done.28), channel_id=1, replica_groups=mesh['dp'=8,'ctx'=4] {'dp'}, dimensions={0}, use_global_device_ids=true | all-gather | bytes 18432 | tf_op jit(solution)/shard_map/all_gather | solution.py:112
  570.9 204.0 %all-gather.21.cloned.1.call-done = bf16[2048,8192]{1,0:T(8,128)(2,1)} async-done(((bf16[256,8192]{1,0:T(8,128)(2,1)}), bf16[2048,8192]{1,0:T(8,128)(2,1)}) %all-gather.21.cloned.1.call-update) | async-done | bytes 33554448 | tf_op jit(solution)/shard_map/all_gather | solution.py:111
  774.9 15.4 convolution_add_fusion
  790.3 2.0 copy-done.16
  792.3 20.8 convolution_convert_fusion.1
  813.4 250.0 %all-gather.23.cloned.1.call-done = bf16[8192,2048]{1,0:T(8,128)(2,1)} async-done(((bf16[1024,2048]{1,0:T(8,128)(2,1)}), bf16[8192,2048]{1,0:T(8,128)(2,1)}) %all-gather.23.cloned.1.call-update) | async-done | bytes 33554448 | tf_op jit(solution)/shard_map/all_gather | solution.py:113
  1063.4 25.0 %fusion.82 = (bf16[8192]{0:T(1024)(128)(2,1)S(1)}, bf16[128,8192]{1,0:T(8,128)(2,1)S(1)}) fusion(f32[128,8192]{1,0:T(8,128)} %copy-done.16, bf16[8192,2048]{1,0:T(8,128)(2,1)} %all-gather.23.cloned.1.call-done, bf16[1,128,2048]{2,1,0:T(8,128)(2,1)S(1)} %copy-done.5), kind=kOutput, calls=%fused_computation.152 | convolution fusion | flops 4371505152 | bytes 40386560 | tf_op jit(solution)/shard_map/dot_general | solution.py:72
  1088.4 14.0 convolution_convert_fusion
  1102.5 49.0 %reduce-scatter.13.cloned.1.call-done = bf16[256,2048]{1,0:T(8,128)(2,1)} async-done(((bf16[2048,2048]{1,0:T(8,128)(2,1)}), bf16[256,2048]{1,0:T(8,128)(2,1)}) %reduce-scatter.13.cloned.1.call-update) | async-done | bytes 1048592 | tf_op jit(solution)/shard_map/reduce_scatter | solution.py:283
  1151.5 247.7 %reduce-scatter.11.cloned.1.call-done = bf16[256,6144]{1,0:T(8,128)(2,1)} async-done(((bf16[2048,6144]{1,0:T(8,128)(2,1)}), bf16[256,6144]{1,0:T(8,128)(2,1)}) %reduce-scatter.11.cloned.1.call-update) | async-done | bytes 3145744 | tf_op jit(solution)/shard_map/reduce_scatter | solution.py:277
  1399.2 326.3 %reduce-scatter.17.cloned.1.call-done = bf16[1024,2048]{1,0:T(8,128)(2,1)} async-done(((bf16[8192,2048]{1,0:T(8,128)(2,1)}), bf16[1024,2048]{1,0:T(8,128)(2,1)}) %reduce-scatter.17.cloned.1.call-update) | async-done | bytes 4194320 | tf_op jit(solution)/shard_map/reduce_scatter | solution.py:214
  1725.5 326.3 %reduce-scatter.15.cloned.1.call-done = bf16[256,8192]{1,0:T(8,128)(2,1)} async-done(((bf16[2048,8192]{1,0:T(8,128)(2,1)}), bf16[256,8192]{1,0:T(8,128)(2,1)}) %reduce-scatter.15.cloned.1.call-update) | async-done | bytes 4194320 | tf_op jit(solution)/shard_map/reduce_scatter | solution.py:208
  2055.2 11.8 all-gather.7
  2067.0 9.9 all-gather.4
  2076.9 6.3 fusion.7
  2083.7 17.7 fusion.83
  2101.4 14.4 fusion.76
  2116.7 22.9 all-reduce.7
  2140.0 8.8 all-reduce.8
  2152.3 1.5 fusion.46
  2153.7 21.2 fusion.9
  2175.0 123.4 %all-reduce.12.cloned.1.call-done = (bf16[256,6144]{1,0:T(8,128)(2,1)}, bf16[256,2048]{1,0:T(8,128)(2,1)}, bf16[256,8192]{1,0:T(8,128)(2,1)}, bf16[1024,2048]{1,0:T(8,128)(2,1)}) async-done(((bf16[256,6144]{1,0:T(8,128)(2,1)}, bf16[256,2048]{1,0:T(8,128)(2,1)}, bf16[256,8192]{1,0:T(8,128)(2,1)}, bf16[1024,2048]{1,0:T(8,128)(2,1)}), (bf16[256,6144]{1,0:T(8,128)(2,1)}, bf16[256,2048]{1,0:T(8,128)(2,1)}, ...) | async-done | bytes 12582928 | tf_op jit(solution)/shard_map/psum | solution.py:294
  2298.3 2.9 convert_element_type.282
  2301.3 3.4 convert_element_type.279
  2304.7 4.4 convert_element_type.285
  2309.1 4.4 convert_element_type.288
  (174 shorter events, 24.7 us)
Async XLA Ops:
  7.2 1.6 copy-start.34
  7.2 1.6 copy-start.35
  7.2 1.6 copy-start.29
  7.2 41.7 %copy-start.33 = (s32[4]{0:T(128)S(1)}, s32[4]{0:T(128)}, u32[]{:S(2)}) copy-start(s32[4]{0:T(128)} %param.17) | copy-start | bytes 52
  7.2 42.4 %copy-start = (bf16[1,128,2048]{2,1,0:T(8,128)(2,1)S(1)}, bf16[1,128,2048]{2,1,0:T(8,128)(2,1)}, u32[]{:S(2)}) copy-start(bf16[1,128,2048]{2,1,0:T(8,128)(2,1)} %param.15) | copy-start | bytes 1572868
  7.2 225.1 %all-gather.15.cloned.1.call-start = ((), (), s32[]{:S(2)}) async-start(), calls=%async_computation.6 | async-start | bytes 28311552 | tf_op jit(solution)/shard_map/all_gather | solution.py:107
  8.0 306.2 %all-gather.19.cloned.1.call-start = ((), (), s32[]{:S(2)}) async-start(), calls=%async_computation.8 | async-start | bytes 9437184 | tf_op jit(solution)/shard_map/all_gather | solution.py:109
  8.7 341.2 %all-gather.17.cloned.1.call-start = ((), (), s32[]{:S(2)}) async-start(), calls=%async_computation.7 | async-start | bytes 2621440 | tf_op jit(solution)/shard_map/all_gather | solution.py:148
  49.0 194.1 %copy-start.25 = (s32[512]{0:T(512)}, s32[512]{0:T(512)S(1)}, u32[]{:S(2)}) copy-start(s32[512]{0:T(512)S(1)} %fusion.59) | copy-start | bytes 6148
  49.8 193.4 %copy-start.21 = (f32[128]{0:T(128)}, f32[128]{0:T(128)S(1)}, u32[]{:S(2)}) copy-start(f32[128]{0:T(128)S(1)} %broadcast_multiply_fusion.1) | copy-start | bytes 1540
  50.1 193.1 %copy-start.30 = (f32[128]{0:T(128)}, f32[128]{0:T(128)S(1)}, u32[]{:S(2)}) copy-start(f32[128]{0:T(128)S(1)} %fusion.39) | copy-start | bytes 1540
  50.1 193.1 %copy-start.23 = (f32[128]{0:T(128)}, f32[128]{0:T(128)S(1)}, u32[]{:S(2)}) copy-start(f32[128]{0:T(128)S(1)} %fusion.66) | copy-start | bytes 1540
  51.1 194.4 %copy-start.20 = (f32[128,32]{1,0:T(8,128)}, f32[128,32]{1,0:T(8,128)S(1)}, u32[]{:S(2)}) copy-start(f32[128,32]{1,0:T(8,128)S(1)} %get-tuple-element.68) | copy-start | bytes 49156
  243.2 1.7 copy-start.1
  245.5 68.7 %copy-start.5 = (bf16[1,128,2048]{2,1,0:T(8,128)(2,1)S(1)}, bf16[1,128,2048]{2,1,0:T(8,128)(2,1)}, u32[]{:S(2)}) copy-start(bf16[1,128,2048]{2,1,0:T(8,128)(2,1)} %param.16) | copy-start | bytes 1572868
  246.6 4.5 copy-start.26
  246.6 4.5 copy-start.27
  248.7 138.8 %all-gather.25.cloned.1.call-start = ((), (), s32[]{:S(2)}) async-start(), calls=%async_computation.15 | async-start | bytes 2621440 | tf_op jit(solution)/shard_map/all_gather | solution.py:149
  250.9 194.2 %reduce-scatter.19.cloned.1.call-start = ((), (), s32[]{:S(2)}) async-start(), calls=%async_computation.16 | async-start | bytes 2621440
  390.3 1.5 copy-start.13
  390.3 1.5 copy-start.18
  390.8 1.0 copy-start.3
  409.7 74.2 %reduce-scatter.21.cloned.1.call-start = ((), (), s32[]{:S(2)}) async-start(), calls=%async_computation.17 | async-start | bytes 2621440
  428.7 346.1 %all-gather.21.cloned.1.call-start = ((), (), s32[]{:S(2)}) async-start(), calls=%async_computation.9 | async-start | bytes 37748736 | tf_op jit(solution)/shard_map/all_gather | solution.py:111
  429.5 633.9 %all-gather.23.cloned.1.call-start = ((), (), s32[]{:S(2)}) async-start(), calls=%async_computation.10 | async-start | bytes 37748736 | tf_op jit(solution)/shard_map/all_gather | solution.py:113
  430.3 721.3 %reduce-scatter.13.cloned.1.call-start = ((), (), s32[]{:S(2)}) async-start(), calls=%async_computation.12 | async-start | bytes 9437184 | tf_op jit(solution)/shard_map/reduce_scatter | solution.py:283
  433.4 0.8 copy-start.6
  440.0 1.2 copy-start.4
  440.0 959.2 %reduce-scatter.11.cloned.1.call-start = ((), (), s32[]{:S(2)}) async-start(), calls=%async_computation.11 | async-start | bytes 28311552 | tf_op jit(solution)/shard_map/reduce_scatter | solution.py:277
  448.7 4.5 copy-start.19
  454.0 52.6 %copy-start.9 = (bf16[1,128,8,256]{1,3,2,0:T(8,128)(2,1)}, bf16[1,128,8,256]{1,3,2,0:T(8,128)(2,1)S(1)}, u32[]{:S(2)}) copy-start(bf16[1,128,8,256]{1,3,2,0:T(8,128)(2,1)S(1)} %copy.94) | copy-start | bytes 1572868
  486.5 20.0 copy-start.7
  487.6 18.9 copy-start.11
  506.5 0.7 copy-start.36
  506.5 0.7 copy-start.37
  506.5 28.2 %copy-start.28 = (bf16[1024]{0:T(1024)(128)(2,1)S(1)}, bf16[1024]{0:T(1024)(128)(2,1)}, u32[]{:S(2)}) copy-start(bf16[1024]{0:T(1024)(128)(2,1)} %param.27) | copy-start | bytes 6148
  506.6 268.3 %copy-start.22 = (f32[128]{0:T(128)S(1)}, f32[128]{0:T(128)}, u32[]{:S(2)}) copy-start(f32[128]{0:T(128)} %copy-done.21) | copy-start | bytes 1540
  506.6 268.3 %copy-start.24 = (f32[128]{0:T(128)S(1)}, f32[128]{0:T(128)}, u32[]{:S(2)}) copy-start(f32[128]{0:T(128)} %copy-done.23) | copy-start | bytes 1540
  506.6 1218.9 %reduce-scatter.17.cloned.1.call-start = ((), (), s32[]{:S(2)}) async-start(), calls=%async_computation.14 | async-start | bytes 37748736 | tf_op jit(solution)/shard_map/reduce_scatter | solution.py:214
  790.3 2.0 copy-start.16
  813.1 1238.7 %reduce-scatter.15.cloned.1.call-start = ((), (), s32[]{:S(2)}) async-start(), calls=%async_computation.13 | async-start | bytes 37748736 | tf_op jit(solution)/shard_map/reduce_scatter | solution.py:208
  1102.5 1195.9 %all-reduce.12.cloned.1.call-start = ((), (), s32[]{:S(2)}) async-start(), calls=%async_computation.18 | async-start | bytes 25165824 | tf_op jit(solution)/shard_map/psum | solution.py:294
  2051.8 0.7 copy-start.40
  2051.8 3.2 copy-start.38
  2051.8 3.2 copy-start.39
  2076.9 6.4 copy-start.8
  2076.9 6.3 copy-start.10
  2076.9 6.3 copy-start.12
  2101.4 14.4 copy-start.31
  2101.4 14.4 copy-start.2
  2149.4 164.2 %copy-start.32 = (f32[256]{0:T(256)}, f32[256]{0:T(256)S(1)}, u32[]{:S(2)}) copy-start(f32[256]{0:T(256)S(1)} %convert_element_type.283) | copy-start | bytes 3076
  2298.3 2.9 copy-start.17
  2301.3 3.5 copy-start.15
  2304.7 4.4 copy-start.14
Sparse Core Ops, SparseCore 0:
  9.7 222.6 all-gather.14
  234.0 80.1 all-gather.18
  316.6 33.2 all-gather.16
  352.2 35.3 all-gather.24
  409.9 35.1 reduce-scatter.18
  448.8 35.1 reduce-scatter.20
  485.6 289.2 all-gather.20
  776.5 286.8 all-gather.22
  1066.2 85.2 reduce-scatter.12
  1153.7 245.4 reduce-scatter.10
  1401.6 323.8 reduce-scatter.16
  1727.9 323.8 reduce-scatter.14
  2055.7 242.5 all-reduce.11
where the time goes:
time: 2330 us; the launch traced here: 2320 us
  waiting for transfers between devices  1860 us (80%)
  matrix products  193 us (8%)
  blocking collectives  157 us (7%)
  local copies, waits for them, and re-layouts  60.4 us (3%)
  other arithmetic  30.4 us (1%)
    reduce_scatter x1, waiting for transfers between devices, local(): lax.psum_scatter(mlp_terms[2].astype(jnp.bfloat16), 'dp', scatter_dimensi...  326 us
    reduce_scatter x1, waiting for transfers between devices, local(): lax.psum_scatter(mlp_terms[0].astype(jnp.bfloat16), 'dp', scatter_dimensi...  326 us
    all_gather x1, waiting for transfers between devices, local(): lax.all_gather(w_down, 'dp', axis=0, tiled=True)  250 us
    reduce_scatter x1, waiting for transfers between devices, local(): lax.psum_scatter(attn_terms[0].astype(jnp.bfloat16), 'dp', scatter_dimens...  248 us
    all_gather x1, waiting for transfers between devices, local(): lax.all_gather(w_up, 'dp', axis=0, tiled=True)  204 us
    all_gather x1, waiting for transfers between devices, local(): lax.all_gather(w_qkv, 'dp', axis=0, tiled=True)  181 us
    psum x1, waiting for transfers between devices, local(): lax.psum(shortened(mlp_shares + attn_shares), 'ctx')  123 us
    dot_general x4, matrix products, contract_cols(): lax.dot_general(left, right, (((1,), (1,)), ((), ())), preferred_element_...  63.3 us
  transfers between devices with their start and end apart: 13, of which 13 were waited for; matrix products, arithmetic and copies ran while one was open for 10% of the time, Pallas kernels for 0%

commit v1 on v0

--- a/solution.py
+++ b/solution.py
@@ -1,6 +1,8 @@
 import jax
 import jax.numpy as jnp
 from jax import lax
+from jax.experimental import pallas as pl
+from jax.experimental.pallas import tpu as pltpu
 from jax.sharding import PartitionSpec as P
 
 H = 8
@@ -74,7 +76,7 @@
     )
 
 
-def local(
+def plain_local(
     tokens,
     cotangent,
     pair_index,
@@ -324,7 +326,883 @@
     )
 
 
+PLANES = 4
+
+
+def hop_line(part, step, first):
+    planes = [z for z in range(PLANES) if 0 <= z + step < PLANES]
+    planes = [z for z in planes if (z if step > 0 else PLANES - 1 - z) >= first]
+    pairs = [(2 * z + k, 2 * (z + step) + k) for z in planes for k in range(2)]
+    return lax.ppermute(part, "dp", pairs)
+
+
+def hop_plane(part, shift):
+    pairs = [(2 * z + k, 2 * ((z + shift) % PLANES) + k) for z in range(PLANES) for k in range(2)]
+    return lax.ppermute(part, "dp", pairs)
+
+
+def hop_core(part):
+    return lax.ppermute(part, "dp", [(d, d ^ 1) for d in range(2 * PLANES)])
+
+
+def hop_ctx(part, flip):
+    return lax.ppermute(part, "ctx", [(c, c ^ flip) for c in range(4)])
+
+
+def pick(stacked, index):
+    return lax.dynamic_index_in_dim(stacked, index, 0, keepdims=False)
+
+
+def in_order(bit, mine, other):
+    return jnp.stack([jnp.where(bit == 0, mine, other), jnp.where(bit == 0, other, mine)])
+
+
+def line_scatter(blocks, z):
+    def block(index):
+        return pick(blocks, jnp.clip(index, 0, PLANES - 1)).astype(jnp.float32)
+
+    total = block(z)
+    for step in (1, -1):
+        flow = None
+        for ahead in (3, 2, 1):
+            own = block(z + step * ahead)
+            flow = own if flow is None else own + flow.astype(jnp.float32)
+            planes = [p for p in range(PLANES) if 0 <= p + step * ahead < PLANES]
+            pairs = [(2 * p + k, 2 * (p + step) + k) for p in planes for k in range(2)]
+            flow = lax.ppermute(flow.astype(jnp.bfloat16), "dp", pairs)
+        total = total + flow.astype(jnp.float32)
+    return total
+
+
+def core_sum(parts, k):
+    low = parts.astype(jnp.bfloat16)
+    return pick(low, k).astype(jnp.float32) + hop_core(pick(low, 1 - k)).astype(jnp.float32)
+
+
+def hop_pair(part):
+    pairs = []
+    for z in range(PLANES):
+        for x in range(2):
+            one, two = (2 * z) * 4 + 2 + x, (2 * z + 1) * 4 + x
+            pairs += [(one, two), (two, one)]
+    return lax.ppermute(part, ("dp", "ctx"), pairs)
+
+
+def dp_exchange(parts, z, core):
+    split = parts.reshape((PLANES, 2) + parts.shape[1:])
+    got = [pick(split, z)]
+    for shift in range(1, PLANES):
+        got.append(hop_plane(pick(split, (z + shift) % PLANES), shift))
+    stacked = jnp.stack([got[0], got[3], got[2], got[1]])
+    lined = jnp.concatenate([stacked, stacked])
+    lined = lax.dynamic_slice_in_dim(lined, (PLANES - z) % PLANES, PLANES)
+    mine = lax.dynamic_index_in_dim(lined, core, 1, keepdims=False)
+    away = lax.dynamic_index_in_dim(lined, 1 - core, 1, keepdims=False)
+    both = in_order(core, mine, hop_core(away))
+    return jnp.swapaxes(both, 0, 1).reshape(parts.shape)
+
+
+MESH_ID = pl.DeviceIdType.MESH
+
+
+def gather_kernel(
+    x_in,
+    g_in,
+    up_in,
+    qkv_in,
+    small_in,
+    x_out,
+    g_out,
+    up_out,
+    qkv_out,
+    small_out,
+    line_send,
+    line_recv,
+    side_send,
+    side_recv,
+    pair_send,
+    core_send,
+    core_recv,
+    w_send,
+    w_recv,
+    wx_send,
+    wx_recv,
+    wy_send,
+    wy_recv,
+    wc_send,
+    wc_recv,
+    small_send,
+    small_recv,
+    local_sem,
+):
+    dp = lax.axis_index("dp")
+    rank = lax.axis_index("ctx")
+    z, k = dp // 2, dp % 2
+    y, x = rank // 2, rank % 2
+    core_to = (2 * z + 1 - k, rank)
+    x_to = (dp, 2 * y + 1 - x)
+    y_to = (dp, 2 * (1 - y) + x)
+    pair_to = (2 * z + 1 - k, 2 * (1 - y) + x)
+    ff_part = up_out.shape[2]
+    dh = qkv_out.shape[2] // 3
+
+    barrier = pltpu.get_barrier_semaphore()
+    for target in (core_to, x_to, y_to, pair_to):
+        pl.semaphore_signal(barrier, inc=1, device_id=target, device_id_type=MESH_ID)
+    for shift in range(1, PLANES):
+        for c in range(2):
+            target = (2 * lax.rem(z + shift, PLANES) + c, rank)
+            pl.semaphore_signal(barrier, inc=1, device_id=target, device_id_type=MESH_ID)
+    pl.semaphore_wait(barrier, 4 + 2 * (PLANES - 1))
+
+    def remote(src, dst, send, recv, target):
+        return pltpu.make_async_remote_copy(
+            src_ref=src,
+            dst_ref=dst,
+            send_sem=send,
+            recv_sem=recv,
+            device_id=target,
+            device_id_type=MESH_ID,
+        )
+
+    arrays = ((g_in, g_out), (x_in, x_out))
+    mine = 2 * k + x
+    theirs = 2 * k + 1 - x
+    sends = []
+
+    def start(copy, when=None):
+        if when is None:
+            copy.start()
+        else:
+            pl.when(when)(copy.start)
+        sends.append((when, copy))
+
+    same = k == y
+    for a, (src, dst) in enumerate(arrays):
+        pair = remote(src, dst.at[z, 2 * y + x], pair_send.at[a], line_recv.at[a, z], pair_to)
+        local = pltpu.make_async_copy(src, dst.at[z, mine], local_sem.at[a])
+        pl.when(jnp.logical_not(same))(pair.start)
+        pl.when(same)(local.start)
+
+    small_local = pltpu.make_async_copy(small_in, small_out.at[dp], local_sem.at[2])
+    small_local.start()
+    small_copies = []
+    for n, (shift, c) in enumerate([(s, c) for s in range(PLANES) for c in range(2)][1:]):
+        target = (2 * lax.rem(z + shift, PLANES) + lax.rem(k + c, 2), rank)
+        copy = remote(
+            small_in, small_out.at[dp], small_send.at[n], small_recv.at[n], target
+        )
+        copy.start()
+        small_copies.append(copy)
+
+    for a, (src, dst) in enumerate(arrays):
+        pair = remote(src, dst.at[z, mine], pair_send.at[a], line_recv.at[a, z], pair_to)
+        local = pltpu.make_async_copy(src, dst.at[z, mine], local_sem.at[a])
+        pl.when(jnp.logical_not(same))(pair.wait_recv)
+        pl.when(same)(local.wait)
+
+    quarter = up_in.shape[0] // 4
+    half = up_in.shape[0] // 2
+    own_copies = []
+    core_copies = []
+
+    def up_cols(target):
+        return up_in.at[:, pl.ds(pl.multiple_of(target * ff_part, 128), ff_part)]
+
+    def qkv_cols(target, section):
+        first = section * qkv_in.shape[1] // 3
+        return qkv_in.at[:, pl.ds(pl.multiple_of(first + target * dh, 128), dh)]
+
+    own_copies.append(pltpu.make_async_copy(up_cols(dp), up_out.at[dp], local_sem.at[3]))
+    core_copies.append(
+        remote(up_cols(2 * z + 1 - k), up_out.at[dp], wc_send.at[0], wc_recv.at[0], core_to)
+    )
+    for section in range(3):
+        columns = pl.ds(section * dh, dh)
+        own_copies.append(
+            pltpu.make_async_copy(
+                qkv_cols(dp, section), qkv_out.at[dp, :, columns], local_sem.at[4 + section]
+            )
+        )
+        core_copies.append(
+            remote(
+                qkv_cols(2 * z + 1 - k, section),
+                qkv_out.at[dp, :, columns],
+                wc_send.at[1 + section],
+                wc_recv.at[1 + section],
+                core_to,
+            )
+        )
+    for copy in own_copies:
+        copy.start()
+
+    def carry(a, plane, when, along):
+        dst = arrays[a][1]
+        block = dst.at[plane, mine]
+        if along in (0, 1):
+            start(
+                remote(block, block, line_send.at[a, 0, plane], line_recv.at[a, plane], (dp + 2, rank)),
+                jnp.logical_and(when, z < PLANES - 1),
+            )
+        if along in (0, -1):
+            start(
+                remote(block, block, line_send.at[a, 1, plane], line_recv.at[a, plane], (dp - 2, rank)),
+                jnp.logical_and(when, z > 0),
+            )
+        start(remote(block, block, side_send.at[a, plane], side_recv.at[a, plane], x_to), when)
+        start(
+            remote(block, block, core_send.at[a, 0, plane], core_recv.at[a, 0, plane], core_to), when
+        )
+
+    def arrived(a, plane, when):
+        block = arrays[a][1].at[plane, mine]
+        copy = remote(block, block, line_send.at[a, 0, plane], line_recv.at[a, plane], core_to)
+        pl.when(when)(copy.wait_recv)
+
+    def side_on(a, plane, when):
+        block = arrays[a][1].at[plane, theirs]
+        copy = remote(block, block, side_send.at[a, plane], side_recv.at[a, plane], core_to)
+        pl.when(when)(copy.wait_recv)
+        start(
+            remote(block, block, core_send.at[a, 1, plane], core_recv.at[a, 1, plane], core_to), when
+        )
+
+    always = z >= 0
+    for a in range(2):
+        carry(a, z, always, 0)
+
+    w_copies = []
+    up_rows = pl.ds(pl.multiple_of(rank * quarter, 16), quarter)
+    qkv_rows = pl.ds(pl.multiple_of(y * half, 16), half)
+    for shift in range(1, PLANES):
+        plane = lax.rem(z + shift, PLANES)
+        for c in range(2):
+            target = (2 * plane + c, rank)
+            columns = pl.ds(pl.multiple_of(target[0] * ff_part, 128), ff_part)
+            w_copies.append(
+                remote(
+                    up_in.at[up_rows, columns],
+                    up_out.at[dp, up_rows],
+                    w_send.at[shift - 1, c, 0],
+                    w_recv.at[shift - 1, k, 0],
+                    target,
+                )
+            )
+            for section in range(3):
+                first = section * qkv_in.shape[1] // 3
+                columns = pl.ds(pl.multiple_of(first + target[0] * dh, 128), dh)
+                w_copies.append(
+                    remote(
+                        qkv_in.at[qkv_rows, columns],
+                        qkv_out.at[dp, qkv_rows, pl.ds(section * dh, dh)],
+                        w_send.at[shift - 1, c, 1 + section],
+                        w_recv.at[shift - 1, k, 1 + section],
+                        target,
+                    )
+                )
+    for copy in w_copies:
+        copy.start()
+    for copy in core_copies:
+        copy.start()
+
+    def w_arrive(shift, c, part):
+        source = 2 * lax.rem(z - shift + PLANES, PLANES) + c
+        if part == 0:
+            dst = up_out.at[source, up_rows]
+        else:
+            dst = qkv_out.at[source, qkv_rows, pl.ds((part - 1) * dh, dh)]
+        remote(dst, dst, w_send.at[shift - 1, c, part], w_recv.at[shift - 1, c, part], core_to).wait_recv()
+
+    def x_rows(flip):
+        other = 2 * y + (1 - x if flip else x)
+        return pl.ds(pl.multiple_of(other * quarter, 16), quarter)
+
+    def pair_of(shift):
+        return pl.ds(2 * lax.rem(z - shift + PLANES, PLANES), 2)
+
+    def share_weights(shift):
+        for c in range(2):
+            for part in range(4):
+                w_arrive(shift, c, part)
+        block = up_out.at[pair_of(shift), up_rows]
+        start(remote(block, block, wx_send.at[shift - 1], wx_recv.at[shift - 1], x_to))
+        start(remote(block, block, wy_send.at[shift - 1, 0], wy_recv.at[shift - 1, 0], y_to))
+        block = qkv_out.at[pair_of(shift), qkv_rows]
+        start(remote(block, block, wy_send.at[shift - 1, 2], wy_recv.at[shift - 1, 2], y_to))
+
+    def share_side_weights(shift):
+        block = up_out.at[pair_of(shift), x_rows(True)]
+        remote(block, block, wx_send.at[shift - 1], wx_recv.at[shift - 1], x_to).wait_recv()
+        start(remote(block, block, wy_send.at[shift - 1, 1], wy_recv.at[shift - 1, 1], y_to))
+
+    for step in range(1, PLANES):
+        for a in range(2):
+            for along in (1, -1):
+                plane = z - along * step
+                there = jnp.logical_and(plane >= 0, plane < PLANES)
+                plane = lax.rem(plane + PLANES, PLANES)
+                arrived(a, plane, there)
+                carry(a, plane, there, along)
+        if step == 1:
+            for a in range(2):
+                side_on(a, z, always)
+        else:
+            for a in range(2):
+                for along in (1, -1):
+                    plane = z - along * (step - 1)
+                    there = jnp.logical_and(plane >= 0, plane < PLANES)
+                    side_on(a, lax.rem(plane + PLANES, PLANES), there)
+        if step > 1:
+            share_weights(step - 1)
+        if step > 2:
+            share_side_weights(step - 2)
+    for a in range(2):
+        for along in (1, -1):
+            plane = z - along * (PLANES - 1)
+            there = jnp.logical_and(plane >= 0, plane < PLANES)
+            side_on(a, lax.rem(plane + PLANES, PLANES), there)
+    share_weights(3)
+    share_side_weights(2)
+    share_side_weights(3)
+
+    for shift in range(1, PLANES):
+        other_y = 2 * (1 - y)
+        for n, other in enumerate((other_y + x, other_y + 1 - x)):
+            block = up_out.at[pair_of(shift), pl.ds(pl.multiple_of(other * quarter, 16), quarter)]
+            remote(block, block, wy_send.at[shift - 1, n], wy_recv.at[shift - 1, n], y_to).wait_recv()
+        block = qkv_out.at[pair_of(shift), pl.ds(pl.multiple_of((1 - y) * half, 16), half)]
+        remote(block, block, wy_send.at[shift - 1, 2], wy_recv.at[shift - 1, 2], y_to).wait_recv()
+    for a in range(2):
+        for plane in range(PLANES):
+            for n, side in enumerate((x, 1 - x)):
+                block = arrays[a][1].at[plane, 2 * (1 - k) + side]
+                remote(
+                    block, block, core_send.at[a, n, plane], core_recv.at[a, n, plane], core_to
+                ).wait_recv()
+    for n, (shift, c) in enumerate([(s, c) for s in range(PLANES) for c in range(2)][1:]):
+        source = 2 * lax.rem(z - shift + PLANES, PLANES) + lax.rem(k + c, 2)
+        remote(
+            small_in, small_out.at[source], small_send.at[n], small_recv.at[n], core_to
+        ).wait_recv()
+    for copy in core_copies:
+        copy.wait()
+    for copy in own_copies:
+        copy.wait()
+    small_local.wait()
+    for copy in small_copies + w_copies:
+        copy.wait_send()
+    for a, (src, dst) in enumerate(arrays):
+        pair = remote(src, dst.at[z, 2 * y + x], pair_send.at[a], line_recv.at[a, z], pair_to)
+        pl.when(jnp.logical_not(same))(pair.wait_send)
+    for when, copy in sends:
+        if when is None:
+            copy.wait_send()
+        else:
+            pl.when(when)(copy.wait_send)
+
+
+def gather_all(tokens, cotangent, w_up, w_qkv, small):
+    rows, width = tokens.shape
+    n_dp = 2 * PLANES
+    bf16 = jnp.bfloat16
+    dma = pltpu.SemaphoreType.DMA
+    hbm = pl.BlockSpec(memory_space=pl.ANY)
+    block = jax.ShapeDtypeStruct((PLANES, 4, rows, width), bf16)
+    return pl.pallas_call(
+        gather_kernel,
+        out_shape=(
+            block,
+            block,
+            jax.ShapeDtypeStruct((n_dp, w_up.shape[0], w_up.shape[1] // n_dp), bf16),
+            jax.ShapeDtypeStruct((n_dp, w_qkv.shape[0], w_qkv.shape[1] // n_dp), bf16),
+            jax.ShapeDtypeStruct((n_dp,) + small.shape, bf16),
+        ),
+        in_specs=[hbm] * 5,
+        out_specs=(hbm,) * 5,
+        scratch_shapes=[
+            dma((2, 2, PLANES)),
+            dma((2, PLANES)),
+            dma((2, PLANES)),
+            dma((2, PLANES)),
+            dma((2,)),
+            dma((2, 2, PLANES)),
+            dma((2, 2, PLANES)),
+            dma((3, 2, 4)),
+            dma((3, 2, 4)),
+            dma((3,)),
+            dma((3,)),
+            dma((3, 3)),
+            dma((3, 3)),
+            dma((4,)),
+            dma((4,)),
+            dma((7,)),
+            dma((7,)),
+            dma((7,)),
+        ],
+        compiler_params=pltpu.CompilerParams(collective_id=1, has_side_effects=True),
+    )(tokens, cotangent, w_up, w_qkv, small)
+
+
+def dot_nn(left, right):
+    return jnp.dot(left, right, preferred_element_type=jnp.float32)
+
+
+def half_turn(head, cosine, sine):
+    first = head[:, :128]
+    lane = lax.broadcasted_iota(jnp.int32, first.shape, 1)
+    swapped = jnp.where(
+        lane < ROT // 2, pltpu.roll(first, 128 - ROT // 2, 1), pltpu.roll(first, ROT // 2, 1)
+    )
+    return jnp.concatenate([first * cosine + swapped * sine, head[:, 128:]], axis=1)
+
+
+def block_kernel(
+    x_hbm,
+    g_hbm,
+    up,
+    down,
+    qkv,
+    out_w,
+    gains,
+    up_bias,
+    qkv_bias,
+    cosine,
+    sine,
+    place_q,
+    place_k,
+    out_hbm,
+    back_hbm,
+    down_hbm,
+    up_hbm,
+    outw_hbm,
+    qkv_hbm,
+    vec,
+    xb,
+    gb,
+    nm,
+    na,
+    nmh,
+    nah,
+    hid,
+    prg,
+    q,
+    k,
+    v,
+    mg,
+    mix,
+    proj,
+    mean_s,
+    inv_s,
+    kacc,
+    vacc,
+    acc_down,
+    acc_up,
+    acc_out,
+    acc_qkv,
+    stage,
+    load_sem,
+    store_sem,
+):
+    f32, bf16 = jnp.float32, jnp.bfloat16
+    x = lax.axis_index("ctx") % 2
+    seqs, length, width = x_hbm.shape
+    ff = up.shape[1]
+    row_tile = 64
+    quarter = length // 4
+    scale = DH ** (-0.5)
+
+    def ds(start, size):
+        return pl.ds(pl.multiple_of(start, size), size)
+
+    def load(s, slot):
+        return (
+            pltpu.make_async_copy(x_hbm.at[s], xb.at[slot], load_sem.at[0, slot]),
+            pltpu.make_async_copy(g_hbm.at[s], gb.at[slot], load_sem.at[1, slot]),
+        )
+
+    def stores(s):
+        return (
+            pltpu.make_async_copy(stage.at[0], out_hbm.at[s], store_sem.at[0]),
+            pltpu.make_async_copy(stage.at[1], back_hbm.at[s], store_sem.at[1]),
+        )
+
+    for copy in load(0, 0):
+        copy.start()
+    for ref in (acc_down, acc_up, acc_out, acc_qkv):
+        rows = ref.shape[0] // 64
+
+        @pl.loop(0, rows)
+        def clear(i, ref=ref):
+            ref[ds(i * 64, 64), :] = jnp.zeros((64, ref.shape[1]), f32)
+
+    vec[...] = jnp.zeros_like(vec)
+
+    @pl.loop(0, seqs)
+    def sequence(s):
+        slot = lax.rem(s, 2)
+        for copy in load(s, slot):
+            copy.wait()
+
+        @pl.when(s + 1 < seqs)
+        def ahead():
+            for copy in load(s + 1, 1 - slot):
+                copy.start()
+
+        @pl.loop(0, length // row_tile)
+        def norm(i):
+            r = ds(i * row_tile, row_tile)
+            value = xb[slot, r, :].astype(f32)
+            mean = jnp.mean(value, axis=1, keepdims=True)
+            centre = value - mean
+            inv = lax.rsqrt(jnp.mean(centre * centre, axis=1, keepdims=True) + EPS_NORM)
+            hat = centre * inv
+            mean_s[r, :] = mean
+            inv_s[r, :] = inv
+            na[r, :] = (hat * gains[0:1, :] + gains[1:2, :]).astype(bf16)
+            nm[r, :] = (hat * gains[2:3, :] + gains[3:4, :]).astype(bf16)
+
+        for d in range(width // 256):
+            nmh[:, d * 128 : (d + 1) * 128] = nm[:, ds(d * 256 + x * 128, 128)]
+            nah[:, d * 128 : (d + 1) * 128] = na[:, ds(d * 256 + x * 128, 128)]
+
+        @pl.loop(0, ff // 256)
+        def feed(n):
+            c = ds(n * 256, 256)
+            pre = dot_nn(nm[...], up[:, c]) + up_bias[:, c]
+            hidden_grad = contract_cols(gb[slot], down[c, :])
+            cdf = 0.5 * (1.0 + lax.erf(pre * (0.5**0.5)))
+            pdf = jnp.exp(-0.5 * pre * pre) * ((2.0 * 3.141592653589793) ** -0.5)
+            hid[:, c] = (pre * cdf).astype(bf16)
+            prg[:, c] = (hidden_grad * (cdf + pre * pdf)).astype(bf16)
+
+        @pl.loop(0, ff // 512)
+        def gdown(m):
+            r = ds(m * 256, 256)
+            acc_down[r, :] += contract_rows(hid[:, ds(x * (ff // 2) + m * 256, 256)], gb[slot])
+
+        @pl.loop(0, width // 512)
+        def gup(m):
+            r = ds(m * 256, 256)
+            acc_up[r, :] += contract_rows(nmh[:, r], prg[...])
+
+        for n, ref in enumerate((q, k, v)):
+            part = dot_nn(na[...], qkv[:, n * DH : (n + 1) * DH]) + qkv_bias[:, n * DH : (n + 1) * DH]
+            if n < 2:
+                part = half_turn(part, cosine[...], sine[...])
+            ref[...] = part.astype(bf16)
+        mg[...] = contract_cols(gb[slot], out_w[...]).astype(bf16)
+        kacc[...] = jnp.zeros_like(kacc)
+        vacc[...] = jnp.zeros_like(vacc)
+
+        @pl.loop(0, 4)
+        def attend(i):
+            r = ds(i * quarter, quarter)
+            scores = contract_cols(q[r, :], k[...]) * scale
+            scores = jnp.where(place_k[...] <= place_q[r, :], scores, MASK_FILL)
+            exponent = jnp.exp(scores - jnp.max(scores, axis=1, keepdims=True))
+            prob = exponent / jnp.sum(exponent, axis=1, keepdims=True)
+            low = prob.astype(bf16)
+            mix[r, :] = dot_nn(low, v[...]).astype(bf16)
+            prob_grad = contract_cols(mg[r, :], v[...])
+            row_dot = jnp.sum(prob_grad * prob, axis=1, keepdims=True)
+            score_grad = (prob * (prob_grad - row_dot)).astype(bf16)
+            query_grad = dot_nn(score_grad, k[...]) * scale
+            proj[r, 0:DH] = half_turn(query_grad, cosine[r, :], -sine[r, :]).astype(bf16)
+            kacc[...] += contract_rows(score_grad, q[r, :])
+            vacc[...] += contract_rows(low, mg[r, :])
+
+        proj[:, DH : 2 * DH] = half_turn(kacc[...] * scale, cosine[...], -sine[...]).astype(bf16)
+        proj[:, 2 * DH : 3 * DH] = vacc[...].astype(bf16)
+        acc_out[...] += contract_rows(mix[:, ds(x * 128, 128)], gb[slot])
+
+        @pl.loop(0, width // 512)
+        def gqkv(m):
+            r = ds(m * 256, 256)
+            acc_qkv[r, :] += contract_rows(nah[:, r], proj[...])
+
+        one, two = ds(x * quarter, quarter), ds((2 + x) * quarter, quarter)
+
+        def picked(ref):
+            return jnp.concatenate([ref[one, :], ref[two, :]], axis=0)
+
+        @pl.when(s > 0)
+        def stored():
+            for copy in stores(s - 1):
+                copy.wait()
+
+        hid_rows, prg_rows = picked(hid), picked(prg)
+        mix_rows, proj_rows = picked(mix), picked(proj)
+        mean_rows, inv_rows = picked(mean_s), picked(inv_s)
+
+        @pl.loop(0, width // 256)
+        def followers(n):
+            c = ds(n * 256, 256)
+            out = dot_nn(picked(hid), down[:, c]) + dot_nn(picked(mix), out_w[:, c])
+            stage[0, 0, :, c] = out[:quarter].astype(bf16)
+            stage[0, 1, :, c] = out[quarter:].astype(bf16)
+            mlp_back = contract_cols(picked(prg), up[c, :])
+            attn_back = contract_cols(picked(proj), qkv[c, :])
+            rows = jnp.concatenate([xb[slot, one, c], xb[slot, two, c]], axis=0).astype(f32)
+            hat = (rows - picked(mean_s)) * picked(inv_s)
+            back = attn_back * gains[0:1, c] + mlp_back * gains[2:3, c]
+            stage[1, 0, :, c] = back[:quarter].astype(bf16)
+            stage[1, 1, :, c] = back[quarter:].astype(bf16)
+            grad = jnp.concatenate([gb[slot, one, c], gb[slot, two, c]], axis=0).astype(f32)
+            sums = (attn_back * hat, attn_back, mlp_back * hat, mlp_back, grad)
+            for n_sum, term in enumerate(sums):
+                vec[n_sum : n_sum + 1, c] += jnp.sum(term, axis=0, keepdims=True)
+
+        vec[5:6, 0 : 3 * DH] += jnp.sum(picked(proj).astype(f32), axis=0, keepdims=True)
+        vec[6:7, 0:ff] += jnp.sum(picked(prg).astype(f32), axis=0, keepdims=True)
+        for copy in stores(s):
+            copy.start()
+
+    for copy in stores(seqs - 1):
+        copy.wait()
+
+    copies = []
+    for ref, buf, target, rows in (
+        (acc_down, xb.at[0], down_hbm, 512),
+        (acc_up, xb.at[1], up_hbm, 512),
+        (acc_qkv, gb.at[0], qkv_hbm, 512),
+        (acc_out, gb.at[1], outw_hbm, 128),
+    ):
+        cols = ref.shape[1]
+        for piece in range(ref.shape[0] // rows):
+
+            @pl.loop(0, rows // 64)
+            def rounded(i, ref=ref, buf=buf, piece=piece, rows=rows, cols=cols):
+                buf[ds(i * 64, 64), piece * cols : (piece + 1) * cols] = ref[
+                    ds(piece * rows + i * 64, 64), :
+                ].astype(bf16)
+
+            copy = pltpu.make_async_copy(
+                buf.at[0:rows, piece * cols : (piece + 1) * cols],
+                target.at[piece * rows : (piece + 1) * rows],
+                store_sem.at[2 + len(copies)],
+            )
+            copy.start()
+            copies.append(copy)
+    for copy in copies:
+        copy.wait()
+
+
+def block_compute(x_all, g_all, up_cols, w_down, qkv_cols, w_out, gains, up_bias, qkv_bias, place):
+    f32, bf16 = jnp.float32, jnp.bfloat16
+    seqs, length, width = x_all.shape
+    ff = up_cols.shape[1]
+    tok = length // 4
+    half_rot = ROT // 2
+    frequency = ROPE_BASE ** (-2.0 * jnp.arange(half_rot, dtype=f32) / ROT)
+    angles = place.astype(f32)[:, None] * frequency[None, :]
+    rest = jnp.zeros((length, 128 - ROT), f32)
+    cosine = jnp.concatenate([jnp.cos(angles), jnp.cos(angles), rest + 1.0], axis=1)
+    sine = jnp.concatenate([-jnp.sin(angles), jnp.sin(angles), rest], axis=1)
+    hbm = pl.BlockSpec(memory_space=pl.ANY)
+    vmem = pl.BlockSpec(memory_space=pltpu.VMEM)
+
+    def shape(*dims, dtype=bf16):
+        return jax.ShapeDtypeStruct(dims, dtype)
+
+    def buf(*dims, dtype=bf16):
+        return pltpu.VMEM(dims, dtype)
+
+    return pl.pallas_call(
+        block_kernel,
+        out_shape=(
+            shape(seqs, 2, tok, width),
+            shape(seqs, 2, tok, width),
+            shape(ff // 2, width),
+            shape(width // 2, ff),
+            shape(DH // 2, width),
+            shape(width // 2, 3 * DH),
+            shape(8, width, dtype=f32),
+        ),
+        in_specs=[hbm, hbm] + [vmem] * 11,
+        out_specs=(hbm,) * 6 + (vmem,),
+        scratch_shapes=[
+            buf(2, length, width),
+            buf(2, length, width),
+            buf(length, width),
+            buf(length, width),
+            buf(length, width // 2),
+            buf(length, width // 2),
+            buf(length, ff),
+            buf(length, ff),
+            buf(length, DH),
+            buf(length, DH),
+            buf(length, DH),
+            buf(length, DH),
+            buf(length, DH),
+            buf(length, 3 * DH),
+            buf(length, 1, dtype=f32),
+            buf(length, 1, dtype=f32),
+            buf(length, DH, dtype=f32),
+            buf(length, DH, dtype=f32),
+            buf(ff // 2, width, dtype=f32),
+            buf(width // 2, ff, dtype=f32),
+            buf(DH // 2, width, dtype=f32),
+            buf(width // 2, 3 * DH, dtype=f32),
+            buf(2, 2, tok, width),
+            pltpu.SemaphoreType.DMA((2, 2)),
+            pltpu.SemaphoreType.DMA((8,)),
+        ],
+        compiler_params=pltpu.CompilerParams(vmem_limit_bytes=62 * 2**20),
+    )(
+        x_all,
+        g_all,
+        up_cols,
+        w_down,
+        qkv_cols,
+        w_out,
+        gains,
+        up_bias,
+        qkv_bias,
+        cosine,
+        sine,
+        place[:, None],
+        place[None, :],
+    )
+
+
+def column_local(
+    tokens,
+    cotangent,
+    pair_index,
+    norm1_gain,
+    norm1_bias,
+    norm2_gain,
+    norm2_bias,
+    w_qkv,
+    b_qkv,
+    w_out,
+    b_out,
+    w_up,
+    b_up,
+    w_down,
+    b_down,
+):
+    bf16, f32 = jnp.bfloat16, jnp.float32
+    tok_count, width = tokens.shape[1:]
+    n_dp = H
+    dp_rank = lax.axis_index("dp")
+    rank = lax.axis_index("ctx")
+    z, core = dp_rank // 2, dp_rank % 2
+    y, x = rank // 2, rank % 2
+    part = width // n_dp
+    ff_part = w_up.shape[1] // n_dp
+    qkv_part = 3 * DH
+    seq_len = 4 * tok_count
+    place = positions(pair_index, tok_count)
+
+    small = jnp.concatenate(
+        [norm1_gain, norm1_bias, norm2_gain, norm2_bias, b_out, b_down, b_qkv]
+    ).reshape(-1, part)
+    small = jnp.pad(small, ((0, -small.shape[0] % 16), (0, 0)))
+    x_all, g_all, up_cols, qkv_cols, small_all = gather_all(
+        tokens[0], cotangent[0], w_up, w_qkv, small
+    )
+    up_cols = up_cols.reshape(width, ff_part)
+    qkv_cols = qkv_cols.reshape(width, qkv_part)
+    vectors = [small_all[:, i].reshape(width).astype(f32) for i in range(6)]
+    gain1, shift1, gain2, shift2, out_bias, down_bias = vectors
+    qkv_bias_all = small_all[:, 6:9].reshape(3, H, DH).astype(f32)
+    qkv_bias = lax.dynamic_index_in_dim(qkv_bias_all, dp_rank, 1, keepdims=False).reshape(qkv_part)
+
+    gains = jnp.stack([gain1, shift1, gain2, shift2] * 2)
+    out_part, back_part, grad_down, grad_up, grad_out, grad_qkv, vec = block_compute(
+        x_all.reshape(PLANES, seq_len, width),
+        g_all.reshape(PLANES, seq_len, width),
+        up_cols,
+        w_down,
+        qkv_cols,
+        w_out,
+        gains,
+        b_up.astype(f32)[None],
+        qkv_bias[None],
+        place,
+    )
+
+    def to_owner(parts):
+        return line_scatter(core_sum(jnp.swapaxes(parts, 0, 1), core), z)
+
+    def home(block):
+        low = block.astype(bf16)
+        return jnp.where(core == y, low, hop_pair(low)).astype(f32)
+
+    out_sum = home(to_owner(out_part.reshape(PLANES, 2, tok_count, width)))
+    own_rows = tokens[0].astype(f32)
+    output = (own_rows + out_sum + out_bias + down_bias).astype(bf16)[None]
+
+    own_head = (jnp.arange(n_dp) == dp_rank).astype(f32)[:, None]
+    vector_parts = jnp.concatenate(
+        [vec[i].reshape(n_dp, part) for i in range(4)]
+        + [
+            (vec[5, :qkv_part].reshape(3, 1, DH) * own_head[None]).reshape(n_dp, -1),
+            vec[4].reshape(n_dp, part) * own_head,
+            vec[6, :ff_part][None] * own_head,
+        ],
+        axis=1,
+    )
+    vector_len = vector_parts.shape[1]
+    vector_rows = jnp.pad(vector_parts, ((0, 0), (0, -vector_len % width)))
+    vector_rows = vector_rows.reshape(PLANES, 2, -1, width)
+    back_mine = to_owner(jnp.concatenate([back_part, vector_rows], axis=2))
+    vector_mine = back_mine[tok_count:].reshape(-1)[:vector_len]
+    back_sum = home(back_mine[:tok_count])
+    vector_row = vector_mine + hop_ctx(vector_mine, 1)
+    vector_total = vector_row + hop_ctx(vector_row, 2)
+    own_centre = own_rows - jnp.mean(own_rows, axis=-1, keepdims=True)
+    own_inv = lax.rsqrt(jnp.mean(own_centre * own_centre, axis=-1, keepdims=True) + EPS_NORM)
+    own_hat = own_centre * own_inv
+    norm_back = (
+        back_sum
+        - jnp.mean(back_sum, axis=-1, keepdims=True)
+        - own_hat * jnp.mean(back_sum * own_hat, axis=-1, keepdims=True)
+    ) * own_inv
+    input_grad = (cotangent[0].astype(f32) + norm_back).astype(bf16)[None]
+
+    def over_y(low):
+        return (low.astype(f32) + hop_ctx(low, 2).astype(f32)).astype(bf16)
+
+    def row_total(grad):
+        low = over_y(grad)
+        return in_order(x, low, hop_ctx(low, 1)).reshape(-1, grad.shape[1]).astype(f32)
+
+    def column_total(grad):
+        low = dp_exchange(over_y(grad).reshape(n_dp, part // 2, -1), z, core)
+        return in_order(x, low, hop_ctx(low, 1))
+
+    down_total = row_total(grad_down)
+    out_total = row_total(grad_out)
+    up_total = column_total(grad_up).transpose(0, 2, 1, 3).reshape(part, -1).astype(f32)
+    qkv_total = column_total(grad_qkv).reshape(2, n_dp, part // 2, 3, DH)
+    qkv_total = qkv_total.transpose(0, 2, 3, 1, 4).reshape(part, -1).astype(f32)
+
+    cuts = [part, 2 * part, 3 * part, 4 * part, 4 * part + b_qkv.shape[0]]
+    cuts.append(cuts[-1] + part)
+    pieces = jnp.split(vector_total, cuts)
+    gain1_total, shift1_total, gain2_total, shift2_total, qkv_bias_total, bias_total, up_bias_total = pieces
+    return (
+        output,
+        input_grad,
+        gain1_total,
+        shift1_total,
+        gain2_total,
+        shift2_total,
+        qkv_total,
+        qkv_bias_total,
+        out_total,
+        bias_total,
+        up_total,
+        up_bias_total,
+        down_total,
+        bias_total,
+    )
+
+
 def solution(mesh):
+    local = column_local if mesh.shape["dp"] == H and mesh.shape["ctx"] == 4 else plain_local
     placed = (
         P("dp", "ctx", None),
         P("dp", "ctx", None),

time: 2330 us -> 680 us (0.29)
  waiting for transfers between devices: 1860 us -> 203 us
  Pallas kernels: 0 us -> 288 us
  matrix products: 193 us -> 0 us
  blocking collectives: 157 us -> 0 us
  starting transfers between devices: 1.35 us -> 72.1 us
    reduce_scatter x4 -> x0, waiting for transfers between devices: 949 us -> none  [the longest x1 326 us: local(): lax.psum_scatter(mlp_terms[2].astype(jnp.bfloat16), 'dp', scatter_dimensi...]
    all_gather x6 -> x0, waiting for transfers between devices: 760 us -> none  [the longest x1 250 us: local(): lax.all_gather(w_down, 'dp', axis=0, tiled=True)]
    pallas_call x0 -> x2, Pallas kernels: none -> 288 us  [the longest x1 171 us: gather_all(): pl.pallas_call(gather_kernel, out_shape=(block, block, jax.ShapeDtypeStru...]
    ppermute x0 -> x34, waiting for transfers between devices: none -> 203 us  [the longest x10 110 us: hop_ctx(): return lax.ppermute(part, 'ctx', [(c, c ^ flip) for c in range(4)])]
    dot_general x18 -> x0, matrix products: 193 us -> none  [the longest x4 63.3 us: contract_cols(): lax.dot_general(left, right, (((1,), (1,)), ((), ())), preferred_element_...]
    all_gather x8 -> x0, blocking collectives: 125 us -> none  [the longest x1 36.1 us: local(): lax.all_gather(b_up, 'dp', axis=0, tiled=True)]
    psum x1 -> x0, waiting for transfers between devices: 123 us -> none  [local(): lax.psum(shortened(mlp_shares + attn_shares), 'ctx')]
    ppermute x0 -> x34, starting transfers between devices: none -> 72.1 us  [the longest x12 34.9 us: line_scatter(): flow = lax.ppermute(flow.astype(jnp.bfloat16), 'dp', pairs)]
  transfers between devices with their start and end apart: 13 -> 34, of which waited for: 13 -> 11; matrix products, arithmetic and copies ran while one was open for 10% -> 11% of each run, Pallas kernels for 0% -> 0%
where the time goes in v1:
time: 680 us; the launch traced here: 670 us
  Pallas kernels  288 us (42%)
  waiting for transfers between devices  203 us (30%)
  starting transfers between devices  72.1 us (11%)
  local copies, waits for them, and re-layouts  61.7 us (9%)
  other arithmetic  43.7 us (6%)
    pallas_call x1, Pallas kernels, gather_all(): pl.pallas_call(gather_kernel, out_shape=(block, block, jax.ShapeDtypeStru...  171 us
    pallas_call x1, Pallas kernels, block_compute(): pl.pallas_call(block_kernel, out_shape=(shape(seqs, 2, tok, width), shape...  117 us
    ppermute x10, waiting for transfers between devices, hop_ctx(): return lax.ppermute(part, 'ctx', [(c, c ^ flip) for c in range(4)])  110 us
    ppermute x6, waiting for transfers between devices, hop_plane(): return lax.ppermute(part, 'dp', pairs)  56.8 us
    ppermute x12, waiting for transfers between devices, line_scatter(): flow = lax.ppermute(flow.astype(jnp.bfloat16), 'dp', pairs)  36.2 us
    ppermute x12, starting transfers between devices, line_scatter(): flow = lax.ppermute(flow.astype(jnp.bfloat16), 'dp', pairs)  34.9 us
    unnamed x52, local copies, waits for them, and re-layouts  22 us
    ppermute x2, starting transfers between devices, hop_pair(): return lax.ppermute(part, ('dp', 'ctx'), pairs)  14.5 us
  transfers between devices with their start and end apart: 34, of which 11 were waited for; matrix products, arithmetic and copies ran while one was open for 11% of the time, Pallas kernels for 0%

profile of v1, /device:TPU:1, one launch (start us, length us, event | category | flops | bytes accessed | tf_op | source)
XLA Modules:
  0.0 670.1 jit_solution(2079398017403826251)
XLA Ops:
  0.7 0.9 dynamic-update-slice.25
  7.2 170.5 %shard_map.254 = (bf16[4,4,128,2048]{3,2,1,0:T(8,128)(2,1)}, bf16[4,4,128,2048]{3,2,1,0:T(8,128)(2,1)}, bf16[8,256,1024]{2,1,0:T(8,128)(2,1)}, bf16[8,256,768]{2,1,0:T(8,128)(2,1)}, bf16[8,16,256]{2,1,0:T(8,128)(2,1)}) custom-call(bf16[128,2048]{1,0:T(8,128)(2,1)} %bitcast.192, bf16[128,2048]{1,0:T(8,128)(2,1)} %bitcast.206, bf16[256,8192]{1,0:T(8,128)(2,1)} %up_in.1, ...), custom_call_target="tpu_custom_call" | custom-call | tf_op jit(solution)/shard_map/pallas_call | solution.py:711
  177.7 1.1 fusion.53
  178.8 0.9 slice_convert_fusion.1
  183.4 1.0 fusion.40
  184.4 1.0 maximum_maximum_fusion
  185.4 117.1 %shard_map.255 = (bf16[4,2,128,2048]{3,2,1,0:T(8,128)(2,1)}, bf16[4,2,128,2048]{3,2,1,0:T(8,128)(2,1)}, bf16[512,2048]{1,0:T(8,128)(2,1)}, bf16[1024,1024]{1,0:T...) custom-call(bf16[4,512,2048]{2,1,0:T(8,128)(2,1)} %bitcast.195, ...), custom_call_target="tpu_custom_call" | custom-call | tf_op jit(solution)/shard_map/pallas_call | solution.py:1010
  304.2 0.9 slice_reduce_fusion.4
  305.8 4.8 constant_dynamic-update-slice_fusion.8
  311.8 1.8 dynamic-slice_bitcast_fusion
  313.6 3.0 copy.91
  316.6 3.0 collective-permute-start.8
  319.6 1.5 dynamic-slice_bitcast_fusion.1
  321.1 1.5 collective-permute-start.26
  322.7 1.2 add_convert_fusion.3
  324.5 11.9 %collective-permute-done.25 = bf16[128,2048]{1,0:T(8,128)(2,1)S(1)} collective-permute-done((bf16[128,2048]{1,0:T(8,128)(2,1)S(1)}, bf16[128,2048]{1,0:T(8,128)(2,1)S(1)}, u32[]{:S(2)}, u32[]{:S(2)}) %collective-permute-start.25) | collective-permute-done | bytes 524320 | tf_op jit(solution)/shard_map/ppermute | solution.py:349
  336.6 20.3 %collective-permute-done.18 = bf16[1024,768]{1,0:T(8,128)(2,1)} collective-permute-done((bf16[1024,768]{1,0:T(8,128)(2,1)}, bf16[1024,768]{1,0:T(8,128)(2,1)}, u32[]{:S(2)}, u32[]{:S(2)}) %collective-permute-start.18) | collective-permute-done | bytes 1572896 | tf_op jit(solution)/shard_map/ppermute | solution.py:349
  356.8 2.3 add_convert_fusion.2
  359.5 4.0 collective-permute-start.20
  363.5 1.6 bitcast_convert_fusion.1
  365.2 4.4 collective-permute-done.19
  369.6 2.6 collective-permute-start.21
  372.3 23.4 %collective-permute-done.20 = bf16[2,128,768]{2,1,0:T(8,128)(2,1)S(1)} collective-permute-done((bf16[2,128,768]{2,1,0:T(8,128)(2,1)S(1)}, bf16[2,128,768]{2,1,0:T(8,128)(2,1)S(1)}, u32[]{:S(2)}, u32[]{:S(2)}) %collective-permute-start.20) | collective-permute-done | bytes 393248 | tf_op jit(solution)/shard_map/ppermute | solution.py:341
  395.7 2.2 collective-permute-start.32
  398.2 2.5 collective-permute-start.22
  400.7 2.4 convert_add_fusion.1
  403.2 2.9 collective-permute-start.1
  406.2 3.3 add_convert_fusion.1
  409.8 36.8 %collective-permute-done.32 = bf16[512,2048]{1,0:T(8,128)(2,1)S(1)} collective-permute-done((bf16[512,2048]{1,0:T(8,128)(2,1)S(1)}, bf16[512,2048]{1,0:T(8,128)(2,1)S(1)}, u32[]{:S(2)}, u32[]{:S(2)}) %collective-permute-start.32) | collective-permute-done | bytes 2097184 | tf_op jit(solution)/shard_map/ppermute | solution.py:349
  446.6 1.6 collective-permute-start.28
  448.2 0.9 add_convert_fusion
  449.1 1.5 collective-permute-start.29
  450.7 1.5 convert_add_fusion
  453.1 29.0 %collective-permute-done.28 = bf16[2,128,1024]{2,1,0:T(8,128)(2,1)S(1)} collective-permute-done((bf16[2,128,1024]{2,1,0:T(8,128)(2,1)S(1)}, bf16[2,128,1024]{2,1,0:T(8,128)(2,1)S(1)}, u32[]{:S(2)}, u32[]{:S(2)}) %collective-permute-start.28) | collective-permute-done | bytes 524320 | tf_op jit(solution)/shard_map/ppermute | solution.py:341
  482.4 3.1 collective-permute-start.9
  486.6 10.3 %collective-permute-done.9 = bf16[130,2048]{1,0:T(8,128)(2,1)S(1)} collective-permute-done((bf16[130,2048]{1,0:T(8,128)(2,1)S(1)}, bf16[130,2048]{1,0:T(8,128)(2,1)S(1)}, u32[]{:S(2)}, u32[]{:S(2)}) %collective-permute-start.9) | collective-permute-done | bytes 532512 | tf_op jit(solution)/shard_map/ppermute | solution.py:372
  496.9 4.1 collective-permute-start.2
  501.2 1.7 collective-permute-start.30
  503.0 2.0 collective-permute-start.10
  505.1 5.8 collective-permute-done.2
  512.1 10.7 %collective-permute-done.10 = bf16[130,2048]{1,0:T(8,128)(2,1)S(1)} collective-permute-done((bf16[130,2048]{1,0:T(8,128)(2,1)S(1)}, bf16[130,2048]{1,0:T(8,128)(2,1)S(1)}, u32[]{:S(2)}, u32[]{:S(2)}) %collective-permute-start.10) | collective-permute-done | bytes 532512 | tf_op jit(solution)/shard_map/ppermute | solution.py:372
  522.8 4.1 collective-permute-start.3
  528.2 1.3 collective-permute-start.6
  530.0 13.2 %collective-permute-start.11 = (bf16[130,2048]{1,0:T(8,128)(2,1)S(1)}, bf16[130,2048]{1,0:T(8,128)(2,1)S(1)}, u32[]{:S(2)}, u32[]{:S(2)}) collective-permute-start(bf16[130,2048]{1,0:T(8,128)(2,1)S(1)} %get-tuple-element.47), channel_id=1, source_target_pairs={{0,8},{4,12},{8,16},{12,20},{16,24},{20,28},{1,9},{5,13},{9,17},{1... | collective-permute-start | bytes 1597448 | tf_op jit(solution)/shard_map/ppermute | solution.py:372
  543.5 1.3 collective-permute-start.14
  544.8 1.0 fusion.24
  545.8 8.7 %collective-permute-start.7 = (bf16[128,2048]{1,0:T(8,128)(2,1)}, bf16[128,2048]{1,0:T(8,128)(2,1)}, u32[]{:S(2)}, u32[]{:S(2)}) collective-permute-start(bf16[128,2048]{1,0:T(8,128)(2,1)} %fusion.24), channel_id=1, source_target_pairs={{2,4},{4,2},{3,5},{5,3},{10,12},{12,10},{11,13},{13,11},{18,20},{2... | collective-permute-start | bytes 1572872 | tf_op jit(solution)/shard_map/ppermute | solution.py:388
  554.8 9.4 %collective-permute-done.14 = bf16[130,2048]{1,0:T(8,128)(2,1)S(1)} collective-permute-done((bf16[130,2048]{1,0:T(8,128)(2,1)S(1)}, bf16[130,2048]{1,0:T(8,128)(2,1)S(1)}, u32[]{:S(2)}, u32[]{:S(2)}) %collective-permute-start.14) | collective-permute-done | bytes 532512 | tf_op jit(solution)/shard_map/ppermute | solution.py:372
  564.9 41.0 %collective-permute-done.16 = f32[3072]{0:T(1024)S(1)} collective-permute-done((f32[3072]{0:T(1024)S(1)}, f32[3072]{0:T(1024)S(1)}, u32[]{:S(2)}, u32[]{:S(2)}) %collective-permute-start.16) | collective-permute-done | bytes 12320 | tf_op jit(solution)/shard_map/ppermute | solution.py:349
  605.9 0.9 collective-permute-start.17
  606.8 4.7 bitcast_convert_fusion
  611.6 0.9 slice.92
  612.4 5.7 collective-permute-start.15
  620.0 2.0 broadcast_select_fusion.1
  621.9 2.6 copy.95
  624.5 2.6 copy.94
  627.1 5.0 convert_bitcast_fusion.1
  632.1 6.6 copy.96
  638.7 7.5 %reshape.379 = f32[256,6144]{1,0:T(8,128)} reshape(f32[2,128,3,8,256]{4,3,2,1,0:T(8,128)} %copy.96) | data formatting | bytes 12582912 | tf_op jit(solution)/shard_map/convert_element_type | solution.py:1180
  646.2 1.8 convert_reduce_fusion
  648.0 2.8 fusion.32
  650.8 1.9 select_bitcast_fusion.3
  653.2 4.9 copy.98
  658.1 11.2 %copy.100 = f32[32,8,8,1024]{3,1,2,0:T(8,128)} copy(f32[32,8,8,1024]{3,2,1,0:T(8,128)S(1)} %bitcast.189) | data formatting | bytes 16777216
  (162 shorter events, 24.3 us)
Async XLA Ops:
  7.2 173.3 %copy-start.8 = (bf16[1024]{0:T(1024)(128)(2,1)S(1)}, bf16[1024]{0:T(1024)(128)(2,1)}, u32[]{:S(2)}) copy-start(bf16[1024]{0:T(1024)(128)(2,1)} %param.27) | copy-start | bytes 6148
  7.2 173.9 %copy-start.9 = (s32[4]{0:T(128)S(1)}, s32[4]{0:T(128)}, u32[]{:S(2)}) copy-start(s32[4]{0:T(128)} %param.17) | copy-start | bytes 52
  302.5 20.2 %collective-permute-start.24 = (bf16[128,2048]{1,0:T(8,128)(2,1)}, bf16[128,2048]{1,0:T(8,128)(2,1)}, u32[]{:S(2)}, u32[]{:S(2)}) collective-permute-start(bf16[128,2048]{1,0:T(8,128)(2,1)} %get-tuple-element.35), channel_id=1, source_target_pairs={{0,2},{1,3},{2,0},{3,1},{4,6},{5,7},{6,4},{7,5},{8,10},{9,11},{10,... | collective-permute-start | bytes 1572872 | tf_op jit(solution)/shard_map/ppermute | solution.py:349
  313.6 6.0 copy-start.2
  316.6 5.9 copy-start
  316.6 6.1 copy-start.6
  316.6 132.5 %collective-permute-start.8 = (bf16[4,130,2048]{2,0,1:T(4,128)(2,1)}, bf16[4,130,2048]{2,0,1:T(4,128)(2,1)S(1)}, u32[]{:S(2)}, u32[]{:S(2)}) collective-permute-start(bf16[4,130,2048]{2,0,1:T(4,128)(2,1)} %copy.91), channel_id=1, source_target_pairs={{0,4},{4,0},{8,12},{12,8},{16,20},{20,16},{24,28},{28,24},{1,5},{5... | collective-permute-start | bytes 6389768 | tf_op jit(solution)/shard_map/ppermute | solution.py:345
  321.0 79.6 %collective-permute-start = (bf16[4,128,2048]{2,1,0:T(8,128)(2,1)}, bf16[4,128,2048]{2,1,0:T(8,128)(2,1)}, u32[]{:S(2)}, u32[]{:S(2)}) collective-permute-start(bf16[4,128,2048]{2,1,0:T(8,128)(2,1)} %dynamic-slice_bitcast_fusion.1), channel_id=1, source_target_pairs={{0,4},{4,0},{8,12},{12,8},{16,20},{20,16},{24,28},{28,24},{1,5},{5... | collective-permute-start | bytes 6291464 | tf_op jit(solution)/shard_map/ppermute | solution.py:345
  321.1 35.8 %collective-permute-start.18 = (bf16[1024,768]{1,0:T(8,128)(2,1)}, bf16[1024,768]{1,0:T(8,128)(2,1)}, u32[]{:S(2)}, u32[]{:S(2)}) collective-permute-start(bf16[1024,768]{1,0:T(8,128)(2,1)} %get-tuple-element.34), channel_id=1, source_target_pairs={{0,2},{1,3},{2,0},{3,1},{4,6},{5,7},{6,4},{7,5},{8,10},{9,11},{10,... | collective-permute-start | bytes 4718600 | tf_op jit(solution)/shard_map/ppermute | solution.py:349
  321.1 85.1 %collective-permute-start.26 = (bf16[1024,1024]{1,0:T(8,128)(2,1)}, bf16[1024,1024]{1,0:T(8,128)(2,1)}, u32[]{:S(2)}, u32[]{:S(2)}) collective-permute-start(bf16[1024,1024]{1,0:T(8,128)(2,1)} %get-tuple-element.36), channel_id=1, source_target_pairs={{0,2},{1,3},{2,0},{3,1},{4,6},{5,7},{6,4},{7,5},{8,10},{9,11},{10,... | collective-permute-start | bytes 6291464 | tf_op jit(solution)/shard_map/ppermute | solution.py:349
  323.9 12.5 %collective-permute-start.25 = (bf16[128,2048]{1,0:T(8,128)(2,1)S(1)}, bf16[128,2048]{1,0:T(8,128)(2,1)S(1)}, u32[]{:S(2)}, u32[]{:S(2)}) collective-permute-start(bf16[128,2048]{1,0:T(8,128)(2,1)S(1)} %add_convert_fusion.3), channel_id=1, source_target_pairs={{0,1},{1,0},{2,3},{3,2},{4,5},{5,4},{6,7},{7,6},{8,9},{9,8},{10,11... | collective-permute-start | bytes 1572872 | tf_op jit(solution)/shard_map/ppermute | solution.py:349
  359.1 36.6 %copy-start.4 = (bf16[512,2048]{1,0:T(8,128)(2,1)S(1)}, bf16[512,2048]{1,0:T(8,128)(2,1)}, u32[]{:S(2)}) copy-start(bf16[512,2048]{1,0:T(8,128)(2,1)} %get-tuple-element.37) | copy-start | bytes 6291460
  359.2 10.4 %collective-permute-start.19 = (bf16[2,128,768]{2,1,0:T(8,128)(2,1)S(1)}, bf16[2,128,768]{2,1,0:T(8,128)(2,1)S(1)}, u32[]{:S(2)}, u32[]{:S(2)}) collective-permute-start(bf16[2,128,768]{2,1,0:T(8,128)(2,1)S(1)} %get-tuple-element.70), channel_id=1, source_target_pairs={{0,24},{4,28},{8,0},{12,4},{16,8},{20,12},{24,16},{28,20},{1,25},{... | collective-permute-start | bytes 1179656 | tf_op jit(solution)/shard_map/ppermute | solution.py:341
  359.5 36.1 %collective-permute-start.20 = (bf16[2,128,768]{2,1,0:T(8,128)(2,1)S(1)}, bf16[2,128,768]{2,1,0:T(8,128)(2,1)S(1)}, u32[]{:S(2)}, u32[]{:S(2)}) collective-permute-start(bf16[2,128,768]{2,1,0:T(8,128)(2,1)S(1)} %get-tuple-element.69), channel_id=1, source_target_pairs={{0,16},{4,20},{8,24},{12,28},{16,0},{20,4},{24,8},{28,12},{1,17},{... | collective-permute-start | bytes 1179656 | tf_op jit(solution)/shard_map/ppermute | solution.py:341
  369.6 28.4 %collective-permute-start.21 = (bf16[2,128,768]{2,1,0:T(8,128)(2,1)S(1)}, bf16[2,128,768]{2,1,0:T(8,128)(2,1)S(1)}, u32[]{:S(2)}, u32[]{:S(2)}) collective-permute-start(bf16[2,128,768]{2,1,0:T(8,128)(2,1)S(1)} %get-tuple-element.67), channel_id=1, source_target_pairs={{0,8},{4,12},{8,16},{12,20},{16,24},{20,28},{24,0},{28,4},{1,9},{5... | collective-permute-start | bytes 1179656 | tf_op jit(solution)/shard_map/ppermute | solution.py:341
  395.7 5.0 copy-start.3
  395.7 50.9 %collective-permute-start.32 = (bf16[512,2048]{1,0:T(8,128)(2,1)S(1)}, bf16[512,2048]{1,0:T(8,128)(2,1)S(1)}, u32[]{:S(2)}, u32[]{:S(2)}) collective-permute-start(bf16[512,2048]{1,0:T(8,128)(2,1)S(1)} %copy-done.4), channel_id=1, source_target_pairs={{0,2},{1,3},{2,0},{3,1},{4,6},{5,7},{6,4},{7,5},{8,10},{9,11},{10,... | collective-permute-start | bytes 6291464 | tf_op jit(solution)/shard_map/ppermute | solution.py:349
  398.2 103.0 %collective-permute-start.22 = (bf16[4,128,768]{2,1,0:T(8,128)(2,1)S(1)}, bf16[4,128,768]{2,1,0:T(8,128)(2,1)S(1)}, u32[]{:S(2)}, u32[]{:S(2)}) collective-permute-start(bf16[4,128,768]{2,1,0:T(8,128)(2,1)S(1)} %dynamic-slice_bitcast_fusion.3), channel_id=1, source_target_pairs={{0,4},{4,0},{8,12},{12,8},{16,20},{20,16},{24,28},{28,24},{1,5},{5... | collective-permute-start | bytes 2359304 | tf_op jit(solution)/shard_map/ppermute | solution.py:345
  403.2 82.6 %collective-permute-start.1 = (bf16[128,2048]{1,0:T(8,128)(2,1)S(1)}, bf16[128,2048]{1,0:T(8,128)(2,1)S(1)}, u32[]{:S(2)}, u32[]{:S(2)}) collective-permute-start(bf16[128,2048]{1,0:T(8,128)(2,1)S(1)} %get-tuple-element.57), channel_id=1, source_target_pairs={{0,8},{4,12},{1,9},{5,13},{2,10},{6,14},{3,11},{7,15}} | collective-permute-start | bytes 1572872 | tf_op jit(solution)/shard_map/ppermute | solution.py:372
  406.2 44.5 %slice-start = ((s8[4456448]{0:T(1024)(128)(4,1)}), s8[4194304]{0:T(1024)(128)(4,1)S(1)}, s32[]{:S(2)}) async-start(s8[4456448]{0:T(1024)(128)(4,1)} %bitcast.190), calls=%async_computation | async-start | bytes 8388608
  409.5 41.1 %slice-start.1 = ((s8[4456448]{0:T(1024)(128)(4,1)}), s8[262144]{0:T(1024)(128)(4,1)S(1)}, s32[]{:S(2)}) async-start(s8[4456448]{0:T(1024)(128)(4,1)} %bitcast.190), calls=%async_computation.1 | async-start | bytes 524288
  409.7 42.6 %collective-permute-start.27 = (bf16[2,128,1024]{2,1,0:T(8,128)(2,1)S(1)}, bf16[2,128,1024]{2,1,0:T(8,128)(2,1)S(1)}, u32[]{:S(2)}, u32[]{:S(2)}) collective-permute-start(bf16[2,128,1024]{2,1,0:T(8,128)(2,1)S(1)} %get-tuple-element.66), channel_id=1, source_target_pairs={{0,24},{4,28},{8,0},{12,4},{16,8},{20,12},{24,16},{28,20},{1,25},{... | collective-permute-start | bytes 1572872 | tf_op jit(solution)/shard_map/ppermute | solution.py:341
  446.6 35.4 %collective-permute-start.28 = (bf16[2,128,1024]{2,1,0:T(8,128)(2,1)S(1)}, bf16[2,128,1024]{2,1,0:T(8,128)(2,1)S(1)}, u32[]{:S(2)}, u32[]{:S(2)}) collective-permute-start(bf16[2,128,1024]{2,1,0:T(8,128)(2,1)S(1)} %get-tuple-element.65), channel_id=1, source_target_pairs={{0,16},{4,20},{8,24},{12,28},{16,0},{20,4},{24,8},{28,12},{1,17},{... | collective-permute-start | bytes 1572872 | tf_op jit(solution)/shard_map/ppermute | solution.py:341
  449.1 33.2 %collective-permute-start.29 = (bf16[2,128,1024]{2,1,0:T(8,128)(2,1)S(1)}, bf16[2,128,1024]{2,1,0:T(8,128)(2,1)S(1)}, u32[]{:S(2)}, u32[]{:S(2)}) collective-permute-start(bf16[2,128,1024]{2,1,0:T(8,128)(2,1)S(1)} %get-tuple-element.63), channel_id=1, source_target_pairs={{0,8},{4,12},{8,16},{12,20},{16,24},{20,28},{24,0},{28,4},{1,9},{5... | collective-permute-start | bytes 1572872 | tf_op jit(solution)/shard_map/ppermute | solution.py:341
  452.3 50.7 %collective-permute-start.4 = (bf16[128,2048]{1,0:T(8,128)(2,1)S(1)}, bf16[128,2048]{1,0:T(8,128)(2,1)S(1)}, u32[]{:S(2)}, u32[]{:S(2)}) collective-permute-start(bf16[128,2048]{1,0:T(8,128)(2,1)S(1)} %get-tuple-element.58), channel_id=1, source_target_pairs={{24,16},{28,20},{25,17},{29,21},{26,18},{30,22},{27,19},{31,23}} | collective-permute-start | bytes 1572872 | tf_op jit(solution)/shard_map/ppermute | solution.py:372
  482.1 63.7 %collective-permute-start.33 = (bf16[512,2048]{1,0:T(8,128)(2,1)S(1)}, bf16[512,2048]{1,0:T(8,128)(2,1)S(1)}, u32[]{:S(2)}, u32[]{:S(2)}) collective-permute-start(bf16[512,2048]{1,0:T(8,128)(2,1)S(1)} %add_convert_fusion), channel_id=1, source_target_pairs={{0,1},{1,0},{2,3},{3,2},{4,5},{5,4},{6,7},{7,6},{8,9},{9,8},{10,11... | collective-permute-start | bytes 6291464 | tf_op jit(solution)/shard_map/ppermute | solution.py:349
  482.4 14.6 %collective-permute-start.9 = (bf16[130,2048]{1,0:T(8,128)(2,1)S(1)}, bf16[130,2048]{1,0:T(8,128)(2,1)S(1)}, u32[]{:S(2)}, u32[]{:S(2)}) collective-permute-start(bf16[130,2048]{1,0:T(8,128)(2,1)S(1)} %get-tuple-element.49), channel_id=1, source_target_pairs={{0,8},{4,12},{1,9},{5,13},{2,10},{6,14},{3,11},{7,15}} | collective-permute-start | bytes 1597448 | tf_op jit(solution)/shard_map/ppermute | solution.py:372
  485.8 26.2 %collective-permute-start.12 = (bf16[130,2048]{1,0:T(8,128)(2,1)S(1)}, bf16[130,2048]{1,0:T(8,128)(2,1)S(1)}, u32[]{:S(2)}, u32[]{:S(2)}) collective-permute-start(bf16[130,2048]{1,0:T(8,128)(2,1)S(1)} %get-tuple-element.50), channel_id=1, source_target_pairs={{24,16},{28,20},{25,17},{29,21},{26,18},{30,22},{27,19},{31,23}} | collective-permute-start | bytes 1597448 | tf_op jit(solution)/shard_map/ppermute | solution.py:372
  496.9 14.0 %collective-permute-start.2 = (bf16[128,2048]{1,0:T(8,128)(2,1)S(1)}, bf16[128,2048]{1,0:T(8,128)(2,1)S(1)}, u32[]{:S(2)}, u32[]{:S(2)}) collective-permute-start(bf16[128,2048]{1,0:T(8,128)(2,1)S(1)} %fusion.21), channel_id=1, source_target_pairs={{0,8},{4,12},{8,16},{12,20},{1,9},{5,13},{9,17},{13,21},{2,10},{6,... | collective-permute-start | bytes 1572872 | tf_op jit(solution)/shard_map/ppermute | solution.py:372
  501.2 26.9 %collective-permute-start.30 = (bf16[4,128,1024]{2,1,0:T(8,128)(2,1)S(1)}, bf16[4,128,1024]{2,1,0:T(8,128)(2,1)S(1)}, u32[]{:S(2)}, u32[]{:S(2)}) collective-permute-start(bf16[4,128,1024]{2,1,0:T(8,128)(2,1)S(1)} %dynamic-slice_bitcast_fusion.2), channel_id=1, source_target_pairs={{0,4},{4,0},{8,12},{12,8},{16,20},{20,16},{24,28},{28,24},{1,5},{5... | collective-permute-start | bytes 3145736 | tf_op jit(solution)/shard_map/ppermute | solution.py:345
  503.0 19.8 %collective-permute-start.10 = (bf16[130,2048]{1,0:T(8,128)(2,1)S(1)}, bf16[130,2048]{1,0:T(8,128)(2,1)S(1)}, u32[]{:S(2)}, u32[]{:S(2)}) collective-permute-start(bf16[130,2048]{1,0:T(8,128)(2,1)S(1)} %fusion.5), channel_id=1, source_target_pairs={{0,8},{4,12},{8,16},{12,20},{1,9},{5,13},{9,17},{13,21},{2,10},{6,... | collective-permute-start | bytes 1597448 | tf_op jit(solution)/shard_map/ppermute | solution.py:372
  511.2 16.1 %collective-permute-start.5 = (bf16[128,2048]{1,0:T(8,128)(2,1)S(1)}, bf16[128,2048]{1,0:T(8,128)(2,1)S(1)}, u32[]{:S(2)}, u32[]{:S(2)}) collective-permute-start(bf16[128,2048]{1,0:T(8,128)(2,1)S(1)} %get-tuple-element.56), channel_id=1, source_target_pairs={{16,8},{20,12},{24,16},{28,20},{17,9},{21,13},{25,17},{29,21},{18,... | collective-permute-start | bytes 1572872 | tf_op jit(solution)/shard_map/ppermute | solution.py:372
  512.1 107.9 %collective-permute-start.23 = (bf16[8,128,768]{2,1,0:T(8,128)(2,1)S(1)}, bf16[8,128,768]{2,1,0:T(8,128)(2,1)S(1)}, u32[]{:S(2)}, u32[]{:S(2)}) collective-permute-start(bf16[8,128,768]{2,1,0:T(8,128)(2,1)S(1)} %bitcast.203), channel_id=1, source_target_pairs={{0,1},{1,0},{2,3},{3,2},{4,5},{5,4},{6,7},{7,6},{8,9},{9,8},{10,11... | collective-permute-start | bytes 4718600 | tf_op jit(solution)/shard_map/ppermute | solution.py:349
  522.8 20.6 %collective-permute-start.3 = (bf16[128,2048]{1,0:T(8,128)(2,1)S(1)}, bf16[128,2048]{1,0:T(8,128)(2,1)S(1)}, u32[]{:S(2)}, u32[]{:S(2)}) collective-permute-start(bf16[128,2048]{1,0:T(8,128)(2,1)S(1)} %get-tuple-element.55), channel_id=1, source_target_pairs={{0,8},{4,12},{8,16},{12,20},{16,24},{20,28},{1,9},{5,13},{9,17},{1... | collective-permute-start | bytes 1572872 | tf_op jit(solution)/shard_map/ppermute | solution.py:372
  527.3 2.7 collective-permute-start.13
  528.2 15.3 %collective-permute-start.6 = (bf16[128,2048]{1,0:T(8,128)(2,1)S(1)}, bf16[128,2048]{1,0:T(8,128)(2,1)S(1)}, u32[]{:S(2)}, u32[]{:S(2)}) collective-permute-start(bf16[128,2048]{1,0:T(8,128)(2,1)S(1)} %fusion.20), channel_id=1, source_target_pairs={{8,0},{12,4},{16,8},{20,12},{24,16},{28,20},{9,1},{13,5},{17,9},{2... | collective-permute-start | bytes 1572872 | tf_op jit(solution)/shard_map/ppermute | solution.py:372
  530.0 24.8 %collective-permute-start.11 = (bf16[130,2048]{1,0:T(8,128)(2,1)S(1)}, bf16[130,2048]{1,0:T(8,128)(2,1)S(1)}, u32[]{:S(2)}, u32[]{:S(2)}) collective-permute-start(bf16[130,2048]{1,0:T(8,128)(2,1)S(1)} %get-tuple-element.47), channel_id=1, source_target_pairs={{0,8},{4,12},{8,16},{12,20},{16,24},{20,28},{1,9},{5,13},{9,17},{1... | collective-permute-start | bytes 1597448 | tf_op jit(solution)/shard_map/ppermute | solution.py:372
  543.4 107.4 %collective-permute-start.31 = (bf16[8,128,1024]{2,1,0:T(8,128)(2,1)S(1)}, bf16[8,128,1024]{2,1,0:T(8,128)(2,1)}, u32[]{:S(2)}, u32[]{:S(2)}) collective-permute-start(bf16[8,128,1024]{2,1,0:T(8,128)(2,1)S(1)} %bitcast.198), channel_id=1, source_target_pairs={{0,1},{1,0},{2,3},{3,2},{4,5},{5,4},{6,7},{7,6},{8,9},{9,8},{10,11... | collective-permute-start | bytes 6291464 | tf_op jit(solution)/shard_map/ppermute | solution.py:349
  543.5 20.7 %collective-permute-start.14 = (bf16[130,2048]{1,0:T(8,128)(2,1)S(1)}, bf16[130,2048]{1,0:T(8,128)(2,1)S(1)}, u32[]{:S(2)}, u32[]{:S(2)}) collective-permute-start(bf16[130,2048]{1,0:T(8,128)(2,1)S(1)} %fusion.4), channel_id=1, source_target_pairs={{8,0},{12,4},{16,8},{20,12},{24,16},{28,20},{9,1},{13,5},{17,9},{2... | collective-permute-start | bytes 1597448 | tf_op jit(solution)/shard_map/ppermute | solution.py:372
  545.8 102.2 %collective-permute-start.7 = (bf16[128,2048]{1,0:T(8,128)(2,1)}, bf16[128,2048]{1,0:T(8,128)(2,1)}, u32[]{:S(2)}, u32[]{:S(2)}) collective-permute-start(bf16[128,2048]{1,0:T(8,128)(2,1)} %fusion.24), channel_id=1, source_target_pairs={{2,4},{4,2},{3,5},{5,3},{10,12},{12,10},{11,13},{13,11},{18,20},{2... | collective-permute-start | bytes 1572872 | tf_op jit(solution)/shard_map/ppermute | solution.py:388
  564.4 47.2 %copy-start.1 = (f32[130,2048]{1,0:T(8,128)}, f32[130,2048]{1,0:T(8,128)S(1)}, u32[]{:S(2)}) copy-start(f32[130,2048]{1,0:T(8,128)S(1)} %fusion.7) | copy-start | bytes 3194884
  564.5 41.5 %collective-permute-start.16 = (f32[3072]{0:T(1024)S(1)}, f32[3072]{0:T(1024)S(1)}, u32[]{:S(2)}, u32[]{:S(2)}) collective-permute-start(f32[3072]{0:T(1024)S(1)} %slice.79), channel_id=1, source_target_pairs={{0,1},{1,0},{2,3},{3,2},{4,5},{5,4},{6,7},{7,6},{8,9},{9,8},{10,11... | collective-permute-start | bytes 36872 | tf_op jit(solution)/shard_map/ppermute | solution.py:349
  605.9 12.2 %collective-permute-start.17 = (f32[3072]{0:T(1024)S(1)}, f32[3072]{0:T(1024)S(1)}, u32[]{:S(2)}, u32[]{:S(2)}) collective-permute-start(f32[3072]{0:T(1024)S(1)} %slice_add_fusion), channel_id=1, source_target_pairs={{0,2},{1,3},{2,0},{3,1},{4,6},{5,7},{6,4},{7,5},{8,10},{9,11},{10,... | collective-permute-start | bytes 36872 | tf_op jit(solution)/shard_map/ppermute | solution.py:349
  612.4 33.8 %collective-permute-start.15 = (bf16[128,2048]{1,0:T(8,128)(2,1)}, bf16[128,2048]{1,0:T(8,128)(2,1)}, u32[]{:S(2)}, u32[]{:S(2)}) collective-permute-start(bf16[128,2048]{1,0:T(8,128)(2,1)} %slice.92), channel_id=1, source_target_pairs={{2,4},{4,2},{3,5},{5,3},{10,12},{12,10},{11,13},{13,11},{18,20},{2... | collective-permute-start | bytes 1572872 | tf_op jit(solution)/shard_map/ppermute | solution.py:388
  620.0 49.3 %copy-start.7 = (f32[256]{0:T(256)}, f32[256]{0:T(256)S(1)}, u32[]{:S(2)}) copy-start(f32[256]{0:T(256)S(1)} %get-tuple-element.118) | copy-start | bytes 3076
  638.7 9.3 %copy-start.5 = (bf16[1,128,2048]{2,1,0:T(8,128)(2,1)S(1)}, bf16[1,128,2048]{2,1,0:T(8,128)(2,1)}, u32[]{:S(2)}) copy-start(bf16[1,128,2048]{2,1,0:T(8,128)(2,1)} %param.16) | copy-start | bytes 1572868

commit v2 on v1

--- a/solution.py
+++ b/solution.py
@@ -1,3 +1,5 @@
+import functools
+
 import jax
 import jax.numpy as jnp
 from jax import lax
@@ -327,79 +329,6 @@
 
 
 PLANES = 4
-
-
-def hop_line(part, step, first):
-    planes = [z for z in range(PLANES) if 0 <= z + step < PLANES]
-    planes = [z for z in planes if (z if step > 0 else PLANES - 1 - z) >= first]
-    pairs = [(2 * z + k, 2 * (z + step) + k) for z in planes for k in range(2)]
-    return lax.ppermute(part, "dp", pairs)
-
-
-def hop_plane(part, shift):
-    pairs = [(2 * z + k, 2 * ((z + shift) % PLANES) + k) for z in range(PLANES) for k in range(2)]
-    return lax.ppermute(part, "dp", pairs)
-
-
-def hop_core(part):
-    return lax.ppermute(part, "dp", [(d, d ^ 1) for d in range(2 * PLANES)])
-
-
-def hop_ctx(part, flip):
-    return lax.ppermute(part, "ctx", [(c, c ^ flip) for c in range(4)])
-
-
-def pick(stacked, index):
-    return lax.dynamic_index_in_dim(stacked, index, 0, keepdims=False)
-
-
-def in_order(bit, mine, other):
-    return jnp.stack([jnp.where(bit == 0, mine, other), jnp.where(bit == 0, other, mine)])
-
-
-def line_scatter(blocks, z):
-    def block(index):
-        return pick(blocks, jnp.clip(index, 0, PLANES - 1)).astype(jnp.float32)
-
-    total = block(z)
-    for step in (1, -1):
-        flow = None
-        for ahead in (3, 2, 1):
-            own = block(z + step * ahead)
-            flow = own if flow is None else own + flow.astype(jnp.float32)
-            planes = [p for p in range(PLANES) if 0 <= p + step * ahead < PLANES]
-            pairs = [(2 * p + k, 2 * (p + step) + k) for p in planes for k in range(2)]
-            flow = lax.ppermute(flow.astype(jnp.bfloat16), "dp", pairs)
-        total = total + flow.astype(jnp.float32)
-    return total
-
-
-def core_sum(parts, k):
-    low = parts.astype(jnp.bfloat16)
-    return pick(low, k).astype(jnp.float32) + hop_core(pick(low, 1 - k)).astype(jnp.float32)
-
-
-def hop_pair(part):
-    pairs = []
-    for z in range(PLANES):
-        for x in range(2):
-            one, two = (2 * z) * 4 + 2 + x, (2 * z + 1) * 4 + x
-            pairs += [(one, two), (two, one)]
-    return lax.ppermute(part, ("dp", "ctx"), pairs)
-
-
-def dp_exchange(parts, z, core):
-    split = parts.reshape((PLANES, 2) + parts.shape[1:])
-    got = [pick(split, z)]
-    for shift in range(1, PLANES):
-        got.append(hop_plane(pick(split, (z + shift) % PLANES), shift))
-    stacked = jnp.stack([got[0], got[3], got[2], got[1]])
-    lined = jnp.concatenate([stacked, stacked])
-    lined = lax.dynamic_slice_in_dim(lined, (PLANES - z) % PLANES, PLANES)
-    mine = lax.dynamic_index_in_dim(lined, core, 1, keepdims=False)
-    away = lax.dynamic_index_in_dim(lined, 1 - core, 1, keepdims=False)
-    both = in_order(core, mine, hop_core(away))
-    return jnp.swapaxes(both, 0, 1).reshape(parts.shape)
 
 
 MESH_ID = pl.DeviceIdType.MESH
@@ -495,7 +424,8 @@
         copy.start()
         small_copies.append(copy)
 
-    for a, (src, dst) in enumerate(arrays):
+    def own_arrived(a):
+        src, dst = arrays[a]
         pair = remote(src, dst.at[z, mine], pair_send.at[a], line_recv.at[a, z], pair_to)
         local = pltpu.make_async_copy(src, dst.at[z, mine], local_sem.at[a])
         pl.when(jnp.logical_not(same))(pair.wait_recv)
@@ -533,9 +463,6 @@
                 core_to,
             )
         )
-    for copy in own_copies:
-        copy.start()
-
     def carry(a, plane, when, along):
         dst = arrays[a][1]
         block = dst.at[plane, mine]
@@ -568,10 +495,8 @@
         )
 
     always = z >= 0
-    for a in range(2):
-        carry(a, z, always, 0)
-
-    w_copies = []
+    up_copies = []
+    qkv_copies = []
     up_rows = pl.ds(pl.multiple_of(rank * quarter, 16), quarter)
     qkv_rows = pl.ds(pl.multiple_of(y * half, 16), half)
     for shift in range(1, PLANES):
@@ -579,7 +504,7 @@
         for c in range(2):
             target = (2 * plane + c, rank)
             columns = pl.ds(pl.multiple_of(target[0] * ff_part, 128), ff_part)
-            w_copies.append(
+            up_copies.append(
                 remote(
                     up_in.at[up_rows, columns],
                     up_out.at[dp, up_rows],
@@ -591,7 +516,7 @@
             for section in range(3):
                 first = section * qkv_in.shape[1] // 3
                 columns = pl.ds(pl.multiple_of(first + target[0] * dh, 128), dh)
-                w_copies.append(
+                qkv_copies.append(
                     remote(
                         qkv_in.at[qkv_rows, columns],
                         qkv_out.at[dp, qkv_rows, pl.ds(section * dh, dh)],
@@ -600,10 +525,6 @@
                         target,
                     )
                 )
-    for copy in w_copies:
-        copy.start()
-    for copy in core_copies:
-        copy.start()
 
     def w_arrive(shift, c, part):
         source = 2 * lax.rem(z - shift + PLANES, PLANES) + c
@@ -620,13 +541,17 @@
     def pair_of(shift):
         return pl.ds(2 * lax.rem(z - shift + PLANES, PLANES), 2)
 
-    def share_weights(shift):
+    def share_up(shift):
         for c in range(2):
-            for part in range(4):
-                w_arrive(shift, c, part)
+            w_arrive(shift, c, 0)
         block = up_out.at[pair_of(shift), up_rows]
         start(remote(block, block, wx_send.at[shift - 1], wx_recv.at[shift - 1], x_to))
         start(remote(block, block, wy_send.at[shift - 1, 0], wy_recv.at[shift - 1, 0], y_to))
+
+    def share_qkv(shift):
+        for c in range(2):
+            for part in range(1, 4):
+                w_arrive(shift, c, part)
         block = qkv_out.at[pair_of(shift), qkv_rows]
         start(remote(block, block, wy_send.at[shift - 1, 2], wy_recv.at[shift - 1, 2], y_to))
 
@@ -635,35 +560,49 @@
         remote(block, block, wx_send.at[shift - 1], wx_recv.at[shift - 1], x_to).wait_recv()
         start(remote(block, block, wy_send.at[shift - 1, 1], wy_recv.at[shift - 1, 1], y_to))
 
-    for step in range(1, PLANES):
+    def step_blocks(step):
+        blocks = []
+        for along in (1, -1):
+            plane = z - along * step
+            there = jnp.logical_and(plane >= 0, plane < PLANES)
+            blocks.append((along, lax.rem(plane + PLANES, PLANES), there))
+        return blocks
+
+    def line_step(step):
         for a in range(2):
-            for along in (1, -1):
-                plane = z - along * step
-                there = jnp.logical_and(plane >= 0, plane < PLANES)
-                plane = lax.rem(plane + PLANES, PLANES)
+            for along, plane, there in step_blocks(step):
                 arrived(a, plane, there)
                 carry(a, plane, there, along)
-        if step == 1:
-            for a in range(2):
-                side_on(a, z, always)
-        else:
-            for a in range(2):
-                for along in (1, -1):
-                    plane = z - along * (step - 1)
-                    there = jnp.logical_and(plane >= 0, plane < PLANES)
-                    side_on(a, lax.rem(plane + PLANES, PLANES), there)
-        if step > 1:
-            share_weights(step - 1)
-        if step > 2:
-            share_side_weights(step - 2)
+
+    def side_step(step):
+        for a in range(2):
+            for unused, plane, there in step_blocks(step):
+                side_on(a, plane, there)
+
     for a in range(2):
-        for along in (1, -1):
-            plane = z - along * (PLANES - 1)
-            there = jnp.logical_and(plane >= 0, plane < PLANES)
-            side_on(a, lax.rem(plane + PLANES, PLANES), there)
-    share_weights(3)
-    share_side_weights(2)
-    share_side_weights(3)
+        own_arrived(a)
+        carry(a, z, always, 0)
+    for copy in core_copies + own_copies:
+        copy.start()
+    line_step(1)
+    for copy in up_copies:
+        copy.start()
+    for a in range(2):
+        side_on(a, z, always)
+    line_step(2)
+    for copy in qkv_copies:
+        copy.start()
+    side_step(1)
+    share_up(1)
+    share_up(2)
+    line_step(3)
+    side_step(2)
+    share_up(3)
+    for shift in range(1, PLANES):
+        share_side_weights(shift)
+    side_step(3)
+    for shift in range(1, PLANES):
+        share_qkv(shift)
 
     for shift in range(1, PLANES):
         other_y = 2 * (1 - y)
@@ -689,7 +628,7 @@
     for copy in own_copies:
         copy.wait()
     small_local.wait()
-    for copy in small_copies + w_copies:
+    for copy in small_copies + up_copies + qkv_copies:
         copy.wait_send()
     for a, (src, dst) in enumerate(arrays):
         pair = remote(src, dst.at[z, 2 * y + x], pair_send.at[a], line_recv.at[a, z], pair_to)
@@ -770,19 +709,25 @@
     sine,
     place_q,
     place_k,
-    out_hbm,
-    back_hbm,
-    down_hbm,
-    up_hbm,
-    outw_hbm,
-    qkv_hbm,
-    vec,
+    out_sum,
+    back_sum,
+    vec_all,
+    down_tot,
+    up_tot,
+    outw_tot,
+    qkv_tot,
+    na_hbm,
+    hp_hbm,
+    got_down,
+    got_up,
+    got_outw,
+    got_qkv,
+    core_got,
+    plane_got,
     xb,
     gb,
-    nm,
-    na,
-    nmh,
-    nah,
+    hx,
+    half_in,
     hid,
     prg,
     q,
@@ -791,28 +736,95 @@
     mg,
     mix,
     proj,
-    mean_s,
-    inv_s,
+    stat,
     kacc,
     vacc,
     acc_down,
     acc_up,
-    acc_out,
-    acc_qkv,
-    stage,
+    g_down,
+    g_up,
+    g_outw,
+    g_qkv,
+    cb,
+    tmp,
+    vec,
+    vec_got,
     load_sem,
-    store_sem,
+    save_sem,
+    tmp_sem,
+    core_send,
+    core_recv,
+    plane_send,
+    plane_recv,
+    home_send,
+    home_recv,
+    y_send,
+    y_recv,
+    x_send,
+    x_recv,
+    a2a_send,
+    a2a_recv,
+    vec_send,
+    vec_recv,
+    local_sem,
 ):
     f32, bf16 = jnp.float32, jnp.bfloat16
-    x = lax.axis_index("ctx") % 2
+    dp = lax.axis_index("dp")
+    rank = lax.axis_index("ctx")
+    z, core = dp // 2, dp % 2
+    y, x = rank // 2, rank % 2
+    core_to = (2 * z + 1 - core, rank)
+    x_to = (dp, 2 * y + 1 - x)
+    y_to = (dp, 2 * (1 - y) + x)
+    pair_to = (2 * z + 1 - core, 2 * (1 - y) + x)
     seqs, length, width = x_hbm.shape
+    tok = length // 4
     ff = up.shape[1]
     row_tile = 64
-    quarter = length // 4
+    half_part = width // (4 * PLANES)
+    section_cols = qkv_tot.shape[1] // 3
     scale = DH ** (-0.5)
-
-    def ds(start, size):
-        return pl.ds(pl.multiple_of(start, size), size)
+    n_qkv = 3 * DH
+
+    barrier = pltpu.get_barrier_semaphore()
+    for target in (core_to, x_to, y_to, pair_to):
+        pl.semaphore_signal(barrier, inc=1, device_id=target, device_id_type=MESH_ID)
+    for shift in range(1, PLANES):
+        for c in range(2):
+            target = (2 * lax.rem(z + shift, PLANES) + c, rank)
+            pl.semaphore_signal(barrier, inc=1, device_id=target, device_id_type=MESH_ID)
+    pl.semaphore_wait(barrier, 4 + 2 * (PLANES - 1))
+
+    def ds(first, size, step=None):
+        return pl.ds(pl.multiple_of(first, step or size), size)
+
+    def remote(src, dst, send, recv, target):
+        return pltpu.make_async_remote_copy(
+            src_ref=src,
+            dst_ref=dst,
+            send_sem=send,
+            recv_sem=recv,
+            device_id=target,
+            device_id_type=MESH_ID,
+        )
+
+    pending = []
+
+    def start(copy, when=None):
+        if when is None:
+            copy.start()
+        else:
+            pl.when(when)(copy.start)
+        pending.append((when, copy.wait_send))
+
+    def start_local(copy, when=None):
+        if when is None:
+            copy.start()
+        else:
+            pl.when(when)(copy.start)
+        pending.append((when, copy.wait))
+
+    one, two = ds(x * tok, tok), ds((2 + x) * tok, tok)
 
     def load(s, slot):
         return (
@@ -820,25 +832,40 @@
             pltpu.make_async_copy(g_hbm.at[s], gb.at[slot], load_sem.at[1, slot]),
         )
 
-    def stores(s):
-        return (
-            pltpu.make_async_copy(stage.at[0], out_hbm.at[s], store_sem.at[0]),
-            pltpu.make_async_copy(stage.at[1], back_hbm.at[s], store_sem.at[1]),
-        )
+    def save_norm(s):
+        return pltpu.make_async_copy(hx.at[1], na_hbm.at[s], save_sem.at[0])
+
+    def save_rows(s):
+        copies = []
+        for n, (ref, cols) in enumerate(((hid, pl.ds(0, ff)), (prg, pl.ds(ff, ff)))):
+            for h, rows in enumerate((one, two)):
+                copies.append(
+                    pltpu.make_async_copy(
+                        ref.at[rows],
+                        hp_hbm.at[s, pl.ds(h * tok, tok), cols],
+                        save_sem.at[1 + 2 * n + h],
+                    )
+                )
+        return copies
 
     for copy in load(0, 0):
         copy.start()
-    for ref in (acc_down, acc_up, acc_out, acc_qkv):
-        rows = ref.shape[0] // 64
-
-        @pl.loop(0, rows)
-        def clear(i, ref=ref):
+
+    def clear(ref):
+        @pl.loop(0, ref.shape[0] // 64)
+        def rows(i):
             ref[ds(i * 64, 64), :] = jnp.zeros((64, ref.shape[1]), f32)
 
+    clear(acc_down)
+    clear(acc_up)
     vec[...] = jnp.zeros_like(vec)
 
+    def choose_half(src, slot):
+        for d in range(width // 256):
+            half_in[:, d * 128 : (d + 1) * 128] = src[slot, :, ds(d * 256 + x * 128, 128)]
+
     @pl.loop(0, seqs)
-    def sequence(s):
+    def feed_forward(s):
         slot = lax.rem(s, 2)
         for copy in load(s, slot):
             copy.wait()
@@ -848,33 +875,38 @@
             for copy in load(s + 1, 1 - slot):
                 copy.start()
 
+        @pl.when(s > 0)
+        def saved():
+            save_norm(s - 1).wait()
+            for copy in save_rows(s - 1):
+                copy.wait()
+
         @pl.loop(0, length // row_tile)
         def norm(i):
             r = ds(i * row_tile, row_tile)
             value = xb[slot, r, :].astype(f32)
-            mean = jnp.mean(value, axis=1, keepdims=True)
-            centre = value - mean
+            centre = value - jnp.mean(value, axis=1, keepdims=True)
             inv = lax.rsqrt(jnp.mean(centre * centre, axis=1, keepdims=True) + EPS_NORM)
             hat = centre * inv
-            mean_s[r, :] = mean
-            inv_s[r, :] = inv
-            na[r, :] = (hat * gains[0:1, :] + gains[1:2, :]).astype(bf16)
-            nm[r, :] = (hat * gains[2:3, :] + gains[3:4, :]).astype(bf16)
-
-        for d in range(width // 256):
-            nmh[:, d * 128 : (d + 1) * 128] = nm[:, ds(d * 256 + x * 128, 128)]
-            nah[:, d * 128 : (d + 1) * 128] = na[:, ds(d * 256 + x * 128, 128)]
+            hx[1, r, :] = (hat * gains[0:1, :] + gains[1:2, :]).astype(bf16)
+            hx[0, r, :] = (hat * gains[2:3, :] + gains[3:4, :]).astype(bf16)
+
+        save_norm(s).start()
+        choose_half(hx, 0)
 
         @pl.loop(0, ff // 256)
         def feed(n):
             c = ds(n * 256, 256)
-            pre = dot_nn(nm[...], up[:, c]) + up_bias[:, c]
+            pre = dot_nn(hx[0], up[:, c]) + up_bias[:, c]
             hidden_grad = contract_cols(gb[slot], down[c, :])
             cdf = 0.5 * (1.0 + lax.erf(pre * (0.5**0.5)))
             pdf = jnp.exp(-0.5 * pre * pre) * ((2.0 * 3.141592653589793) ** -0.5)
             hid[:, c] = (pre * cdf).astype(bf16)
             prg[:, c] = (hidden_grad * (cdf + pre * pdf)).astype(bf16)
 
+        for copy in save_rows(s):
+            copy.start()
+
         @pl.loop(0, ff // 512)
         def gdown(m):
             r = ds(m * 256, 256)
@@ -883,20 +915,238 @@
         @pl.loop(0, width // 512)
         def gup(m):
             r = ds(m * 256, 256)
-            acc_up[r, :] += contract_rows(nmh[:, r], prg[...])
-
+            acc_up[r, :] += contract_rows(half_in[:, r], prg[...])
+
+        rows_sum = jnp.sum(prg[one, :].astype(f32), axis=0, keepdims=True)
+        rows_sum += jnp.sum(prg[two, :].astype(f32), axis=0, keepdims=True)
+        vec[0, 6:7, 0:ff] += rows_sum
+
+    save_norm(seqs - 1).wait()
+    for copy in save_rows(seqs - 1):
+        copy.wait()
+
+    def add_rows(dst, src, rows):
+        @pl.loop(0, rows // 32)
+        def tiles(i):
+            r = ds(i * 32, 32)
+            dst[r, :] = (dst[r, :].astype(f32) + src[r, :].astype(f32)).astype(bf16)
+
+    def add_pieces(pieces):
+        copies = []
+        first = 0
+        for n, (dst, src) in enumerate(pieces):
+            rows, cols = dst.shape
+            here = tmp.at[first : first + rows, 0:cols]
+            copy = pltpu.make_async_copy(src, here, tmp_sem.at[n])
+            copy.start()
+            copies.append((copy, dst, here, rows))
+            first += rows
+        for copy, dst, here, rows in copies:
+            copy.wait()
+            add_rows(dst, here, rows)
+
+    down_pieces = g_down.shape[0] // tok
+
+    def y_copy(kind, piece):
+        sems = (y_send.at[kind, piece], y_recv.at[kind, piece])
+        if kind == 0:
+            rows = pl.ds(piece * tok, tok)
+            return remote(g_down.at[rows], got_down.at[rows], *sems, y_to)
+        if kind == 1:
+            return remote(g_outw, got_outw, *sems, y_to)
+        src, got = (g_up, got_up) if kind == 2 else (g_qkv, got_qkv)
+        pair = pl.ds(2 * lax.rem(z + piece, PLANES), 2)
+        return remote(src.at[pair], got.at[pair], *sems, y_to)
+
+    half_rows = ds(x * half_part, half_part)
+    other_half = ds((1 - x) * half_part, half_part)
+
+    def column_parts(kind, index, source):
+        if kind == 2:
+            return [(g_up.at[index], up_tot.at[half_rows, ds(source * ff, ff)])]
+        return [
+            (
+                g_qkv.at[index, :, pl.ds(n * DH, DH)],
+                qkv_tot.at[half_rows, ds(n * section_cols + source * DH, DH)],
+            )
+            for n in range(3)
+        ]
+
+    def side_parts(kind, plane, rows):
+        if kind == 2:
+            return [up_tot.at[rows, ds(plane * 2 * ff, 2 * ff)]]
+        return [qkv_tot.at[rows, ds(n * section_cols + plane * 2 * DH, 2 * DH)] for n in range(3)]
+
+    def reduced(kind, piece):
+        y_copy(kind, piece).wait()
+        if kind == 0:
+            rows = pl.ds(piece * tok, tok)
+            add_pieces([(g_down.at[rows], got_down.at[rows])])
+            place = down_tot.at[ds(x * g_down.shape[0] + piece * tok, tok)]
+            start_local(pltpu.make_async_copy(g_down.at[rows], place, local_sem.at[2 + piece]))
+            start(remote(g_down.at[rows], place, x_send.at[0, piece], x_recv.at[0, piece], x_to))
+            return
+        if kind == 1:
+            add_pieces([(g_outw, got_outw)])
+            place = outw_tot.at[half_rows]
+            start_local(pltpu.make_async_copy(g_outw, place, local_sem.at[6]))
+            start(remote(g_outw, place, x_send.at[1, 0], x_recv.at[1, 0], x_to))
+            return
+        got, own = ((got_up, g_up), (got_qkv, g_qkv))[kind - 2]
+        plane = lax.rem(z + piece, PLANES)
+        add_pieces([(own.at[2 * plane + c], got.at[2 * plane + c]) for c in range(2)])
+        for c in range(2):
+            for part, (src, dst) in enumerate(column_parts(kind, 2 * plane + c, dp)):
+                send = a2a_send.at[kind - 2, piece, c, part]
+                recv = a2a_recv.at[kind - 2, piece, core, part]
+                copy = remote(src, dst, send, recv, (2 * plane + c, rank))
+                if piece == 0:
+                    local = pltpu.make_async_copy(
+                        src, dst, local_sem.at[7 + 3 * (kind - 2) + part]
+                    )
+                    pl.when(core == c)(local.start)
+                    start(copy, core != c)
+                else:
+                    start(copy)
+
+    def share(kind, shift):
+        plane = lax.rem(z - shift + PLANES, PLANES)
+        for c in range(2):
+            for part, (src, dst) in enumerate(column_parts(kind, 2 * plane + c, 2 * plane + c)):
+                recv = a2a_recv.at[kind - 2, shift, c, part]
+                copy = remote(dst, dst, a2a_send.at[kind - 2, shift, c, part], recv, core_to)
+                if shift == 0:
+                    pl.when(core != c)(copy.wait_recv)
+                    local = pltpu.make_async_copy(
+                        src, dst, local_sem.at[7 + 3 * (kind - 2) + part]
+                    )
+                    pl.when(core == c)(local.wait)
+                else:
+                    copy.wait_recv()
+        for part, block in enumerate(side_parts(kind, plane, half_rows)):
+            sems = (x_send.at[kind + part, shift], x_recv.at[kind + part, shift])
+            start(remote(block, block, *sems, x_to))
+
+    order = (0, 3, 2, 1)
+
+    def core_copy(i):
+        s = order[i]
+        return remote(
+            cb.at[seqs + i % 2], core_got.at[s], core_send.at[i], core_recv.at[i], core_to
+        )
+
+    def chip_sum(i):
+        s = order[i]
+        core_copy(i).wait_recv()
+        add_pieces([(cb.at[i, a], core_got.at[s, a]) for a in range(2)])
+        start(flow_copy(i, 0), jnp.logical_and(z == 0, s > 0))
+        start(flow_copy(i, 1), jnp.logical_and(z == PLANES - 1, s < PLANES - 1))
+
+    def flow_copy(i, side):
+        s = order[i]
+        sems = (plane_send.at[i], plane_recv.at[side, s])
+        return remote(cb.at[i], plane_got.at[side, s], *sems, (dp + (2, -2)[side], rank))
+
+    def flow_add(i, side):
+        flow_copy(i, side).wait_recv()
+        add_pieces([(cb.at[i, a], plane_got.at[side, order[i], a]) for a in range(2)])
+
+    def flow_relay(i, hop):
+        s = order[i]
+        for side, plane in enumerate((hop, PLANES - 1 - hop)):
+            if (plane < s) if side == 0 else (plane > s):
+                here = z == plane
+                pl.when(here)(functools.partial(flow_add, i, side))
+                start(flow_copy(i, side), here)
+
+    def flow_end(i):
+        s = order[i]
+
+        @pl.when(z == s)
+        def both():
+            if s > 0:
+                flow_add(i, 0)
+            if s < PLANES - 1:
+                flow_add(i, 1)
+
+        same = core == y
+        for a, result in enumerate((out_sum, back_sum)):
+            block = cb.at[i, a]
+            start_local(
+                pltpu.make_async_copy(block, result, local_sem.at[a]),
+                jnp.logical_and(z == s, same),
+            )
+            start(
+                remote(block, result, home_send.at[a], home_recv.at[a], pair_to),
+                jnp.logical_and(z == s, jnp.logical_not(same)),
+            )
+
+    def rounded(dst, src, rows, cols):
+        @pl.loop(0, rows // 64)
+        def tiles(i):
+            r = ds(i * 64, 64)
+            dst[r, :] = src[r, 0:cols].astype(bf16)
+
+    def rounded_columns(dst, src, cols):
+        @pl.loop(0, dst.shape[0])
+        def blocks(d):
+            dst[d] = src[ds(d * half_part, half_part), 0:cols].astype(bf16)
+
+    def load_again(i, slot):
+        s = order[i]
+        copies = [
+            pltpu.make_async_copy(na_hbm.at[s], xb.at[slot], load_sem.at[0, slot]),
+            pltpu.make_async_copy(g_hbm.at[s], gb.at[slot], load_sem.at[1, slot]),
+            pltpu.make_async_copy(
+                hp_hbm.at[s], hx.at[slot, pl.ds(2 * tok, 2 * tok)], load_sem.at[2, slot]
+            ),
+        ]
+        for h, rows in enumerate((one, two)):
+            copies.append(
+                pltpu.make_async_copy(
+                    x_hbm.at[s, rows],
+                    hx.at[slot, pl.ds(h * tok, tok)],
+                    load_sem.at[3 + h, slot],
+                )
+            )
+        return copies
+
+    for copy in load_again(0, 0):
+        copy.start()
+    rounded(g_down, acc_down, g_down.shape[0], width)
+    for piece in (0, 1):
+        y_copy(0, piece).start()
+    rounded_columns(g_up, acc_up, ff)
+    for shift in (1, 0, 2, 3):
+        y_copy(2, shift).start()
+    for piece in range(2, down_pieces):
+        y_copy(0, piece).start()
+    clear(acc_up)
+    clear(acc_down.at[0 : tok])
+
+    def attention(i, tick):
+        slot = i % 2
+        for copy in load_again(i, slot):
+            copy.wait()
+        if i + 1 < seqs:
+            for copy in load_again(i + 1, 1 - slot):
+                copy.start()
+        tick(i, 0)
+        choose_half(xb, slot)
         for n, ref in enumerate((q, k, v)):
-            part = dot_nn(na[...], qkv[:, n * DH : (n + 1) * DH]) + qkv_bias[:, n * DH : (n + 1) * DH]
+            c = slice(n * DH, (n + 1) * DH)
+            part = dot_nn(xb[slot], qkv[:, c]) + qkv_bias[:, c]
             if n < 2:
                 part = half_turn(part, cosine[...], sine[...])
             ref[...] = part.astype(bf16)
         mg[...] = contract_cols(gb[slot], out_w[...]).astype(bf16)
+        tick(i, 1)
         kacc[...] = jnp.zeros_like(kacc)
         vacc[...] = jnp.zeros_like(vacc)
 
         @pl.loop(0, 4)
-        def attend(i):
-            r = ds(i * quarter, quarter)
+        def attend(part):
+            r = ds(part * tok, tok)
             scores = contract_cols(q[r, :], k[...]) * scale
             scores = jnp.where(place_k[...] <= place_q[r, :], scores, MASK_FILL)
             exponent = jnp.exp(scores - jnp.max(scores, axis=1, keepdims=True))
@@ -913,78 +1163,141 @@
 
         proj[:, DH : 2 * DH] = half_turn(kacc[...] * scale, cosine[...], -sine[...]).astype(bf16)
         proj[:, 2 * DH : 3 * DH] = vacc[...].astype(bf16)
-        acc_out[...] += contract_rows(mix[:, ds(x * 128, 128)], gb[slot])
+        tick(i, 2)
+        acc_down[0:tok, :] += contract_rows(mix[:, ds(x * 128, 128)], gb[slot])
 
         @pl.loop(0, width // 512)
         def gqkv(m):
             r = ds(m * 256, 256)
-            acc_qkv[r, :] += contract_rows(nah[:, r], proj[...])
-
-        one, two = ds(x * quarter, quarter), ds((2 + x) * quarter, quarter)
+            acc_up[r, 0:n_qkv] += contract_rows(half_in[:, r], proj[...])
+
+        tick(i, 3)
+        value = hx[slot, 0 : 2 * tok, :].astype(f32)
+        mean = jnp.mean(value, axis=1, keepdims=True)
+        centre = value - mean
+        stat[0] = mean
+        stat[1] = lax.rsqrt(jnp.mean(centre * centre, axis=1, keepdims=True) + EPS_NORM)
+        if i >= 2:
+            core_copy(i - 2).wait_send()
 
         def picked(ref):
             return jnp.concatenate([ref[one, :], ref[two, :]], axis=0)
 
-        @pl.when(s > 0)
-        def stored():
-            for copy in stores(s - 1):
-                copy.wait()
-
-        hid_rows, prg_rows = picked(hid), picked(prg)
-        mix_rows, proj_rows = picked(mix), picked(proj)
-        mean_rows, inv_rows = picked(mean_s), picked(inv_s)
+        place = [jnp.where(core == h, i, seqs + i % 2) for h in range(2)]
+        later = slice(2 * tok, 4 * tok)
 
         @pl.loop(0, width // 256)
         def followers(n):
             c = ds(n * 256, 256)
-            out = dot_nn(picked(hid), down[:, c]) + dot_nn(picked(mix), out_w[:, c])
-            stage[0, 0, :, c] = out[:quarter].astype(bf16)
-            stage[0, 1, :, c] = out[quarter:].astype(bf16)
-            mlp_back = contract_cols(picked(prg), up[c, :])
+            out = dot_nn(hx[slot, later, 0:ff], down[:, c]) + dot_nn(picked(mix), out_w[:, c])
+            mlp_back = contract_cols(hx[slot, later, ff : 2 * ff], up[c, :])
             attn_back = contract_cols(picked(proj), qkv[c, :])
-            rows = jnp.concatenate([xb[slot, one, c], xb[slot, two, c]], axis=0).astype(f32)
-            hat = (rows - picked(mean_s)) * picked(inv_s)
             back = attn_back * gains[0:1, c] + mlp_back * gains[2:3, c]
-            stage[1, 0, :, c] = back[:quarter].astype(bf16)
-            stage[1, 1, :, c] = back[quarter:].astype(bf16)
+            for h in range(2):
+                rows = slice(h * tok, (h + 1) * tok)
+                cb[place[h], 0, :, c] = out[rows].astype(bf16)
+                cb[place[h], 1, :, c] = back[rows].astype(bf16)
+            hat = (hx[slot, 0 : 2 * tok, c].astype(f32) - stat[0]) * stat[1]
             grad = jnp.concatenate([gb[slot, one, c], gb[slot, two, c]], axis=0).astype(f32)
             sums = (attn_back * hat, attn_back, mlp_back * hat, mlp_back, grad)
             for n_sum, term in enumerate(sums):
-                vec[n_sum : n_sum + 1, c] += jnp.sum(term, axis=0, keepdims=True)
-
-        vec[5:6, 0 : 3 * DH] += jnp.sum(picked(proj).astype(f32), axis=0, keepdims=True)
-        vec[6:7, 0:ff] += jnp.sum(picked(prg).astype(f32), axis=0, keepdims=True)
-        for copy in stores(s):
-            copy.start()
-
-    for copy in stores(seqs - 1):
-        copy.wait()
-
-    copies = []
-    for ref, buf, target, rows in (
-        (acc_down, xb.at[0], down_hbm, 512),
-        (acc_up, xb.at[1], up_hbm, 512),
-        (acc_qkv, gb.at[0], qkv_hbm, 512),
-        (acc_out, gb.at[1], outw_hbm, 128),
-    ):
-        cols = ref.shape[1]
-        for piece in range(ref.shape[0] // rows):
-
-            @pl.loop(0, rows // 64)
-            def rounded(i, ref=ref, buf=buf, piece=piece, rows=rows, cols=cols):
-                buf[ds(i * 64, 64), piece * cols : (piece + 1) * cols] = ref[
-                    ds(piece * rows + i * 64, 64), :
-                ].astype(bf16)
-
-            copy = pltpu.make_async_copy(
-                buf.at[0:rows, piece * cols : (piece + 1) * cols],
-                target.at[piece * rows : (piece + 1) * rows],
-                store_sem.at[2 + len(copies)],
+                vec[0, n_sum : n_sum + 1, c] += jnp.sum(term, axis=0, keepdims=True)
+
+        vec[0, 5:6, 0:n_qkv] += jnp.sum(picked(proj).astype(f32), axis=0, keepdims=True)
+        core_copy(i).start()
+        tick(i, 4)
+
+    plan = {
+        (0, 3): [(reduced, 0, 0)],
+        (1, 1): [(chip_sum, 0)],
+        (1, 2): [(reduced, 0, 1)],
+        (1, 4): [(reduced, 2, 1)],
+        (2, 1): [(chip_sum, 1)],
+        (2, 3): [(reduced, 2, 0), (flow_relay, 0, 1)],
+        (2, 4): [(share, 2, 0), (share, 2, 1)],
+        (3, 1): [(chip_sum, 2), (reduced, 2, 2)],
+        (3, 2): [(flow_relay, 1, 1)],
+        (3, 4): [(reduced, 2, 3), (flow_relay, 0, 2)],
+    }
+
+    def tick(i, point):
+        for step, *which in plan.get((i, point), ()):
+            step(*which)
+
+    for i in range(seqs):
+        attention(i, tick)
+
+    rounded_columns(g_qkv, acc_up, n_qkv)
+    for shift in (1, 2, 3, 0):
+        y_copy(3, shift).start()
+    rounded(g_outw, acc_down, tok, width)
+    y_copy(1, 0).start()
+
+    def vec_copy(n):
+        target = (x_to, y_to)[n]
+        return remote(vec.at[n], vec_got.at[n], vec_send.at[n], vec_recv.at[n], target)
+
+    vec_copy(0).start()
+    chip_sum(3)
+    reduced(0, 2)
+    flow_relay(2, 1)
+    vec_copy(0).wait()
+    vec[1] = vec[0] + vec_got[0]
+    vec_copy(1).start()
+    share(2, 2)
+    flow_relay(1, 2)
+    reduced(0, 3)
+    flow_end(0)
+    vec_copy(1).wait()
+    vec_all[dp] = vec[1] + vec_got[1]
+    peers = [(s, c) for s in range(PLANES) for c in range(2)][1:]
+    for n, (shift, c) in enumerate(peers):
+        target = (2 * lax.rem(z + shift, PLANES) + lax.rem(core + c, 2), rank)
+        start(
+            remote(
+                vec_all.at[dp], vec_all.at[dp], vec_send.at[2 + n], vec_recv.at[2 + n], target
             )
-            copy.start()
-            copies.append(copy)
-    for copy in copies:
-        copy.wait()
+        )
+    share(2, 3)
+    flow_relay(3, 1)
+    reduced(3, 1)
+    flow_end(2)
+    reduced(3, 2)
+    flow_end(1)
+    share(3, 1)
+    reduced(3, 3)
+    flow_end(3)
+    reduced(3, 0)
+    share(3, 2)
+    share(3, 0)
+    reduced(1, 0)
+    share(3, 3)
+
+    for n, (shift, c) in enumerate(peers):
+        source = 2 * lax.rem(z - shift + PLANES, PLANES) + lax.rem(core + c, 2)
+        block = vec_all.at[source]
+        remote(block, block, vec_send.at[2 + n], vec_recv.at[2 + n], core_to).wait_recv()
+    for piece in range(down_pieces):
+        block = down_tot.at[ds((1 - x) * g_down.shape[0] + piece * tok, tok)]
+        remote(block, block, x_send.at[0, piece], x_recv.at[0, piece], x_to).wait_recv()
+    block = outw_tot.at[other_half]
+    remote(block, block, x_send.at[1, 0], x_recv.at[1, 0], x_to).wait_recv()
+    for kind in (2, 3):
+        for shift in range(PLANES):
+            plane = lax.rem(z - shift + PLANES, PLANES)
+            for part, block in enumerate(side_parts(kind, plane, other_half)):
+                sems = (x_send.at[kind + part, shift], x_recv.at[kind + part, shift])
+                remote(block, block, *sems, x_to).wait_recv()
+    for a, result in enumerate((out_sum, back_sum)):
+        copy = remote(result, result, home_send.at[a], home_recv.at[a], pair_to)
+        pl.when(core != y)(copy.wait_recv)
+    for i in range(seqs - 2, seqs):
+        core_copy(i).wait_send()
+    for when, wait in pending:
+        if when is None:
+            wait()
+        else:
+            pl.when(when)(wait)
 
 
 def block_compute(x_all, g_all, up_cols, w_down, qkv_cols, w_out, gains, up_bias, qkv_bias, place):
@@ -992,6 +1305,8 @@
     seqs, length, width = x_all.shape
     ff = up_cols.shape[1]
     tok = length // 4
+    n_dp = 2 * PLANES
+    half_part = width // (2 * n_dp)
     half_rot = ROT // 2
     frequency = ROPE_BASE ** (-2.0 * jnp.arange(half_rot, dtype=f32) / ROT)
     angles = place.astype(f32)[:, None] * frequency[None, :]
@@ -1000,6 +1315,7 @@
     sine = jnp.concatenate([-jnp.sin(angles), jnp.sin(angles), rest], axis=1)
     hbm = pl.BlockSpec(memory_space=pl.ANY)
     vmem = pl.BlockSpec(memory_space=pltpu.VMEM)
+    dma = pltpu.SemaphoreType.DMA
 
     def shape(*dims, dtype=bf16):
         return jax.ShapeDtypeStruct(dims, dtype)
@@ -1007,25 +1323,31 @@
     def buf(*dims, dtype=bf16):
         return pltpu.VMEM(dims, dtype)
 
-    return pl.pallas_call(
+    results = pl.pallas_call(
         block_kernel,
         out_shape=(
+            shape(tok, width),
+            shape(tok, width),
+            shape(n_dp, 8, width, dtype=f32),
+            shape(ff, width),
+            shape(2 * half_part, n_dp * ff),
+            shape(DH, width),
+            shape(2 * half_part, n_dp * 3 * DH),
+            shape(seqs, length, width),
+            shape(seqs, 2 * tok, 2 * ff),
+            shape(ff // 2, width),
+            shape(n_dp, half_part, ff),
+            shape(DH // 2, width),
+            shape(n_dp, half_part, 3 * DH),
             shape(seqs, 2, tok, width),
-            shape(seqs, 2, tok, width),
-            shape(ff // 2, width),
-            shape(width // 2, ff),
-            shape(DH // 2, width),
-            shape(width // 2, 3 * DH),
-            shape(8, width, dtype=f32),
+            shape(2, seqs, 2, tok, width),
         ),
         in_specs=[hbm, hbm] + [vmem] * 11,
-        out_specs=(hbm,) * 6 + (vmem,),
+        out_specs=(hbm, hbm, vmem) + (hbm,) * 12,
         scratch_shapes=[
             buf(2, length, width),
             buf(2, length, width),
-            buf(length, width),
-            buf(length, width),
-            buf(length, width // 2),
+            buf(2, length, width),
             buf(length, width // 2),
             buf(length, ff),
             buf(length, ff),
@@ -1035,19 +1357,41 @@
             buf(length, DH),
             buf(length, DH),
             buf(length, 3 * DH),
-            buf(length, 1, dtype=f32),
-            buf(length, 1, dtype=f32),
+            buf(2, 2 * tok, 1, dtype=f32),
             buf(length, DH, dtype=f32),
             buf(length, DH, dtype=f32),
             buf(ff // 2, width, dtype=f32),
             buf(width // 2, ff, dtype=f32),
-            buf(DH // 2, width, dtype=f32),
-            buf(width // 2, 3 * DH, dtype=f32),
-            buf(2, 2, tok, width),
-            pltpu.SemaphoreType.DMA((2, 2)),
-            pltpu.SemaphoreType.DMA((8,)),
+            buf(ff // 2, width),
+            buf(n_dp, half_part, ff),
+            buf(DH // 2, width),
+            buf(n_dp, half_part, 3 * DH),
+            buf(seqs + 2, 2, tok, width),
+            buf(2 * tok, width),
+            buf(2, 8, width, dtype=f32),
+            buf(2, 8, width, dtype=f32),
+            dma((5, 2)),
+            dma((5,)),
+            dma((2,)),
+            dma((seqs,)),
+            dma((seqs,)),
+            dma((seqs,)),
+            dma((2, seqs)),
+            dma((2,)),
+            dma((2,)),
+            dma((4, 4)),
+            dma((4, 4)),
+            dma((6, 4)),
+            dma((6, 4)),
+            dma((2, PLANES, 2, 3)),
+            dma((2, PLANES, 2, 3)),
+            dma((9,)),
+            dma((9,)),
+            dma((13,)),
         ],
-        compiler_params=pltpu.CompilerParams(vmem_limit_bytes=62 * 2**20),
+        compiler_params=pltpu.CompilerParams(
+            collective_id=2, has_side_effects=True, vmem_limit_bytes=63 * 2**20
+        ),
     )(
         x_all,
         g_all,
@@ -1063,6 +1407,7 @@
         place[:, None],
         place[None, :],
     )
+    return results[:7]
 
 
 def column_local(
@@ -1110,7 +1455,7 @@
     qkv_bias = lax.dynamic_index_in_dim(qkv_bias_all, dp_rank, 1, keepdims=False).reshape(qkv_part)
 
     gains = jnp.stack([gain1, shift1, gain2, shift2] * 2)
-    out_part, back_part, grad_down, grad_up, grad_out, grad_qkv, vec = block_compute(
+    out_sum, back_sum, vec_all, down_total, up_total, out_total, qkv_total = block_compute(
         x_all.reshape(PLANES, seq_len, width),
         g_all.reshape(PLANES, seq_len, width),
         up_cols,
@@ -1123,35 +1468,10 @@
         place,
     )
 
-    def to_owner(parts):
-        return line_scatter(core_sum(jnp.swapaxes(parts, 0, 1), core), z)
-
-    def home(block):
-        low = block.astype(bf16)
-        return jnp.where(core == y, low, hop_pair(low)).astype(f32)
-
-    out_sum = home(to_owner(out_part.reshape(PLANES, 2, tok_count, width)))
+    back_sum = back_sum.astype(f32)
     own_rows = tokens[0].astype(f32)
-    output = (own_rows + out_sum + out_bias + down_bias).astype(bf16)[None]
-
-    own_head = (jnp.arange(n_dp) == dp_rank).astype(f32)[:, None]
-    vector_parts = jnp.concatenate(
-        [vec[i].reshape(n_dp, part) for i in range(4)]
-        + [
-            (vec[5, :qkv_part].reshape(3, 1, DH) * own_head[None]).reshape(n_dp, -1),
-            vec[4].reshape(n_dp, part) * own_head,
-            vec[6, :ff_part][None] * own_head,
-        ],
-        axis=1,
-    )
-    vector_len = vector_parts.shape[1]
-    vector_rows = jnp.pad(vector_parts, ((0, 0), (0, -vector_len % width)))
-    vector_rows = vector_rows.reshape(PLANES, 2, -1, width)
-    back_mine = to_owner(jnp.concatenate([back_part, vector_rows], axis=2))
-    vector_mine = back_mine[tok_count:].reshape(-1)[:vector_len]
-    back_sum = home(back_mine[:tok_count])
-    vector_row = vector_mine + hop_ctx(vector_mine, 1)
-    vector_total = vector_row + hop_ctx(vector_row, 2)
+    output = (own_rows + out_sum.astype(f32) + out_bias + down_bias).astype(bf16)[None]
+
     own_centre = own_rows - jnp.mean(own_rows, axis=-1, keepdims=True)
     own_inv = lax.rsqrt(jnp.mean(own_centre * own_centre, axis=-1, keepdims=True) + EPS_NORM)
     own_hat = own_centre * own_inv
@@ -1162,27 +1482,16 @@
     ) * own_inv
     input_grad = (cotangent[0].astype(f32) + norm_back).astype(bf16)[None]
 
-    def over_y(low):
-        return (low.astype(f32) + hop_ctx(low, 2).astype(f32)).astype(bf16)
-
-    def row_total(grad):
-        low = over_y(grad)
-        return in_order(x, low, hop_ctx(low, 1)).reshape(-1, grad.shape[1]).astype(f32)
-
-    def column_total(grad):
-        low = dp_exchange(over_y(grad).reshape(n_dp, part // 2, -1), z, core)
-        return in_order(x, low, hop_ctx(low, 1))
-
-    down_total = row_total(grad_down)
-    out_total = row_total(grad_out)
-    up_total = column_total(grad_up).transpose(0, 2, 1, 3).reshape(part, -1).astype(f32)
-    qkv_total = column_total(grad_qkv).reshape(2, n_dp, part // 2, 3, DH)
-    qkv_total = qkv_total.transpose(0, 2, 3, 1, 4).reshape(part, -1).astype(f32)
-
-    cuts = [part, 2 * part, 3 * part, 4 * part, 4 * part + b_qkv.shape[0]]
-    cuts.append(cuts[-1] + part)
-    pieces = jnp.split(vector_total, cuts)
-    gain1_total, shift1_total, gain2_total, shift2_total, qkv_bias_total, bias_total, up_bias_total = pieces
+    totals = jnp.sum(vec_all[:, :4], axis=0)
+    mine = lax.dynamic_slice_in_dim(totals, dp_rank * part, part, 1)
+    gain1_total, shift1_total, gain2_total, shift2_total = mine
+    own_vec = lax.dynamic_index_in_dim(vec_all, dp_rank, 0, keepdims=False)
+    bias_total = lax.dynamic_slice_in_dim(own_vec[4], dp_rank * part, part)
+    up_bias_total = own_vec[6, :ff_part]
+    qkv_bias_total = vec_all[:, 5, :qkv_part].reshape(n_dp, 3, DH).swapaxes(0, 1).reshape(-1)
+    qkv_bias_total = lax.dynamic_slice_in_dim(
+        qkv_bias_total, dp_rank * b_qkv.shape[0], b_qkv.shape[0]
+    )
     return (
         output,
         input_grad,
@@ -1190,13 +1499,13 @@
         shift1_total,
         gain2_total,
         shift2_total,
-        qkv_total,
+        qkv_total.astype(f32),
         qkv_bias_total,
-        out_total,
+        out_total.astype(f32),
         bias_total,
-        up_total,
+        up_total.astype(f32),
         up_bias_total,
-        down_total,
+        down_total.astype(f32),
         bias_total,
     )
 

time: 680 us -> 512 us (0.75); the launches traced: 670 us -> 511 us
  waiting for transfers between devices: 203 us -> 0 us
  Pallas kernels: 288 us -> 472 us
  starting transfers between devices: 72.1 us -> 0 us
  local copies, waits for them, and re-layouts: 61.7 us -> 10.2 us
  other arithmetic: 43.7 us -> 27.8 us
    ppermute x34 -> x0, waiting for transfers between devices: 203 us -> none  [the longest x10 110 us: hop_ctx(): return lax.ppermute(part, 'ctx', [(c, c ^ flip) for c in range(4)])]
    pallas_call x1, Pallas kernels: 117 us -> 308 us  [block_compute(): pl.pallas_call(block_kernel, out_shape=(shape(tok, width), shape(tok, wid...]
    ppermute x34 -> x0, starting transfers between devices: 72.1 us -> none  [the longest x12 34.9 us: line_scatter(): flow = lax.ppermute(flow.astype(jnp.bfloat16), 'dp', pairs)]
    convert_element_type x5 -> x0, local copies, waits for them, and re-layouts: 19.3 us -> none  [the longest x2 14.1 us: column_local(): qkv_total = qkv_total.transpose(0, 2, 3, 1, 4).reshape(part, -1).astype(f32)]
    unnamed x52 -> x24, local copies, waits for them, and re-layouts: 22 us -> 5.63 us
    convert_element_type x16 -> x5, other arithmetic: 21.7 us -> 17.3 us  [the longest x1 6.73 us: column_local(): up_total.astype(f32)]
  transfers between devices with their start and end apart: 34 -> 0, of which waited for: 11 -> 0; matrix products, arithmetic and copies ran while one was open for 11% -> 0% of each run, Pallas kernels for 0% -> 0%
where the time goes in v2:
time: 512 us; the launch traced here: 511 us
  Pallas kernels  472 us (92%)
  other arithmetic  27.8 us (5%)
  local copies, waits for them, and re-layouts  10.2 us (2%)
    pallas_call x1, Pallas kernels, block_compute(): pl.pallas_call(block_kernel, out_shape=(shape(tok, width), shape(tok, wid...  308 us
    pallas_call x1, Pallas kernels, gather_all(): pl.pallas_call(gather_kernel, out_shape=(block, block, jax.ShapeDtypeStru...  164 us

profile of v2, /device:TPU:1, one launch (start us, length us, event | category | flops | bytes accessed | tf_op | source)
XLA Modules:
  0.0 510.6 jit_solution(2802108957204170501)
XLA Ops:
  0.7 0.9 dynamic-update-slice
  1.5 0.8 dynamic-update-slice.1
  2.3 0.8 dynamic-update-slice.2
  3.2 0.8 dynamic-update-slice.3
  4.0 0.8 dynamic-update-slice.4
  4.8 0.8 dynamic-update-slice.5
  5.7 0.8 dynamic-update-slice.6
  6.5 0.6 pad.4.small_in
  7.1 0.0 copy-start.7
  7.2 0.0 copy-start.6
  7.2 163.7 %shard_map.254 = (bf16[4,4,128,2048]{3,2,1,0:T(8,128)(2,1)}, bf16[4,4,128,2048]{3,2,1,0:T(8,128)(2,1)}, bf16[8,256,1024]{2,1,0:T(8,128)(2,1)}, bf16[8,256,768]{2,1,0:T(8,128)(2,1)}, bf16[8,16,256]{2,1,0:T(8,128)(2,1)}) custom-call(bf16[128,2048]{1,0:T(8,128)(2,1)} %bitcast.39, bf16[128,2048]{1,0:T(8,128)(2,1)} %bitcast.44, bf16[256,8192]{1,0:T(8,128)(2,1)} %up_in.1, ...), custom_call_target="tpu_custom_call" | custom-call | tf_op jit(solution)/shard_map/pallas_call | solution.py:650
  170.9 1.1 slice_convert_fusion.2
  172.0 0.1 stack.4
  172.1 0.6 stack.5.gains
  172.8 0.9 slice_convert_fusion
  173.7 0.6 constant_dynamic-slice_fusion.1
  174.2 0.0 copy-done.7
  174.3 0.1 select_reduce_fusion
  174.4 1.0 fusion.21
  175.4 0.1 pad.10.clone
  175.4 0.1 pad.7.clone
  175.5 1.0 maximum_maximum_fusion
  176.5 0.1 copy.38
  176.7 0.8 fusion.15.place_q
  177.4 0.6 fusion.22.place_k
  178.0 0.0 copy-done.6
  178.0 0.6 broadcast_in_dim.46
  178.6 0.0 copy-start
  178.6 308.0 %shard_map.255 = (bf16[128,2048]{1,0:T(8,128)(2,1)}, bf16[128,2048]{1,0:T(8,128)(2,1)}, f32[8,8,2048]{2,1,0:T(8,128)}, bf16[1024,2048]{1,0:T(8,128)(2,1)}, bf16[...) custom-call(bf16[4,512,2048]{2,1,0:T(8,128)(2,1)} %bitcast.40, ...), custom_call_target="tpu_custom_call" | custom-call | tf_op jit(solution)/shard_map/pallas_call | solution.py:1326
  486.7 0.0 copy-start.4
  486.7 0.0 copy-done
  486.7 0.2 convert_reduce_fusion.1
  486.8 0.3 fusion.7
  487.1 1.4 convert_reduce_fusion
  488.6 3.0 fusion.13
  491.6 0.0 copy-done.4
  491.6 0.1 dynamic-slice.6
  491.7 0.0 copy-start.5
  491.7 0.7 fusion.34
  492.4 0.1 slice_reduce_fusion.1
  492.5 0.7 dynamic_slice.21
  493.2 0.6 slice.45
  493.8 0.0 copy-start.1
  493.8 6.7 %convert_element_type.129 = f32[256,8192]{1,0:T(8,128)} convert(bf16[256,8192]{1,0:T(8,128)(2,1)} %get-tuple-element.36) | non-fusion elementwise | flops 2097152 | bytes 12582912 | tf_op jit(solution)/shard_map/convert_element_type | solution.py:1506
  500.5 0.0 copy-done.1
  500.5 0.0 copy-start.2
  500.5 4.4 convert_element_type.130
  505.0 0.0 copy-done.2
  505.0 0.0 copy-start.3
  505.0 3.4 convert_element_type.127
  508.4 0.0 copy-done.3
  508.4 1.6 convert_element_type.128
  510.0 0.0 copy-done.5
  510.0 0.6 copy.51
  (17 shorter events, 0.2 us)
Async XLA Ops:
  7.1 167.1 %copy-start.7 = (s32[4]{0:T(128)S(1)}, s32[4]{0:T(128)}, u32[]{:S(2)}) copy-start(s32[4]{0:T(128)} %param.17) | copy-start | bytes 52
  7.2 170.9 %copy-start.6 = (bf16[1024]{0:T(1024)(128)(2,1)S(1)}, bf16[1024]{0:T(1024)(128)(2,1)}, u32[]{:S(2)}) copy-start(bf16[1024]{0:T(1024)(128)(2,1)} %param.27) | copy-start | bytes 6148
  178.6 308.1 %copy-start = (bf16[1,128,2048]{2,1,0:T(8,128)(2,1)S(1)}, bf16[1,128,2048]{2,1,0:T(8,128)(2,1)}, u32[]{:S(2)}) copy-start(bf16[1,128,2048]{2,1,0:T(8,128)(2,1)} %param.15) | copy-start | bytes 1572868
  486.7 5.0 copy-start.4
  491.7 18.3 %copy-start.5 = (f32[1,1,256]{2,1,0:T(1,128)}, f32[1,1,256]{2,1,0:T(1,128)S(1)}, u32[]{:S(2)}) copy-start(f32[1,1,256]{2,1,0:T(1,128)S(1)} %dynamic-slice.6) | copy-start | bytes 3076
  493.8 6.7 %copy-start.1 = (bf16[1024,2048]{1,0:T(8,128)(2,1)S(1)}, bf16[1024,2048]{1,0:T(8,128)(2,1)}, u32[]{:S(2)}) copy-start(bf16[1024,2048]{1,0:T(8,128)(2,1)} %get-tuple-element.37) | copy-start | bytes 12582916
  500.5 4.5 copy-start.2
  505.0 3.4 copy-start.3
